TPU v7x, 32 devices: a whole 2x2x4 slice. The times are simulated.
32 devices in a mesh: batch: 4 (over y, x), strip: 8 (over z, core).
Axes of the slice: x: 2, y: 2, z: 4, core: 2. Of those that a mesh axis runs over, the one named last changes fastest.
Arguments:
- camera_features: bfloat16 [4, 16896, 256], P('batch', 'strip'), may hold values from -6 to 6
- lidar_bev: bfloat16 [4, 48, 180, 256], P('batch', 'strip'), may hold values from -6 to 6
- pool_index: int32 [4, 16896, 118], P('batch', 'strip'), may hold values from 0 to 8639, as said below
- box_peaks: int32 [4, 3, 150], P('batch'), may hold values from 0 to 179, as said below
- box_count: int32 [4], P('batch'), may hold values from 1 to 150
- w_depth: float32 [256, 198], replicated, may hold values from -1 to 1
- m_depth: float32 [256, 198], replicated, may hold values from -7.6293945e-05 to 7.6293945e-05
- v_depth: float32 [256, 198], replicated, may hold values from 9.864268e-13 to 1.5782828e-11
- w_join: float32 [3, 3, 336, 256], P(None, None, None, 'strip'), may hold values from -0.109375 to 0.109375
- m_join: float32 [3, 3, 336, 256], P(None, None, None, 'strip'), may hold values from -1.9073486e-05 to 1.9073486e-05
- v_join: float32 [3, 3, 336, 256], P(None, None, None, 'strip'), may hold values from 6.458747e-14 to 1.0333995e-12
- w_res: float32 [3, 3, 256, 256], P(None, None, None, 'strip'), may hold values from -0.125 to 0.125
- m_res: float32 [3, 3, 256, 256], P(None, None, None, 'strip'), may hold values from -2.2888184e-05 to 2.2888184e-05
- v_res: float32 [3, 3, 256, 256], P(None, None, None, 'strip'), may hold values from 8.477105e-14 to 1.3563368e-12
- w_head: float32 [256, 10], replicated, may hold values from -0.375 to 0.375
- m_head: float32 [256, 10], replicated, may hold values from -0.00030517578 to 0.00030517578
- v_head: float32 [256, 10], replicated, may hold values from 1.953125e-11 to 3.125e-10
- norm_params: float32 [4, 256], replicated, may hold values from 0.25 to 1.75
- m_norm: float32 [4, 256], replicated, may hold values from -0.00048828125 to 0.00048828125
- v_norm: float32 [4, 256], replicated, may hold values from 4.8828126e-11 to 7.8125e-10
- head_bias: float32 [10], replicated, may hold values from -2.5 to -1.5
- m_bias: float32 [10], replicated, may hold values from -0.0048828125 to 0.0048828125
- v_bias: float32 [10], replicated, may hold values from 5e-09 to 8e-08
Outputs:
- loss: float32 [1], replicated
- grad_norms: float32 [6], replicated
- new_w_depth: float32 [256, 198], replicated
- new_m_depth: float32 [256, 198], replicated
- new_v_depth: float32 [256, 198], replicated
- new_w_join: float32 [3, 3, 336, 256], P(None, None, None, 'strip')
- new_m_join: float32 [3, 3, 336, 256], P(None, None, None, 'strip')
- new_v_join: float32 [3, 3, 336, 256], P(None, None, None, 'strip')
- new_w_res: float32 [3, 3, 256, 256], P(None, None, None, 'strip')
- new_m_res: float32 [3, 3, 256, 256], P(None, None, None, 'strip')
- new_v_res: float32 [3, 3, 256, 256], P(None, None, None, 'strip')
- new_w_head: float32 [256, 10], replicated
- new_m_head: float32 [256, 10], replicated
- new_v_head: float32 [256, 10], replicated
- new_norm: float32 [4, 256], replicated
- new_m_norm: float32 [4, 256], replicated
- new_v_norm: float32 [4, 256], replicated
- new_bias: float32 [10], replicated
- new_m_bias: float32 [10], replicated
- new_v_bias: float32 [10], replicated
Inputs may be any that keep to these rules, and one draw needn't show every extreme that they name: `pool_index`: cell = row * 180 + column of one sample's grid; rows near the middle of the grid are named more often. `box_peaks`: per slot: row below 48, column below 180, class below 10.
All inputs are finite; a program needn't handle non-finite values.
Results may differ from a plain program's by a relative error of at most 0.015.
Values may be sent and summed in bfloat16 or wider, within the bound.
No kernel may reach another device: no remote copies, remote signals or barrier semaphores. Data moves between devices by JAX's collectives and lax.ppermute only.
A program may use at most 192 MiB of HBM per device.

v0:
```python
import functools

import jax
import jax.numpy as jnp
from jax import lax
from jax.experimental import pallas as pl
from jax.experimental.pallas import tpu as pltpu
from jax.sharding import PartitionSpec as P

STEP = 5


EPS_NORM = 1e-05
SPREAD_TWICE = 8.0
SMALL_RATE = 0.25
CLIP_NORM = 0.01
FAR = 1e9


def edges(first, last):
    peers = lax.axis_size("strip")
    up = [(i, i + 1) for i in range(peers - 1)]
    before = lax.ppermute(last, "strip", up)
    after = lax.ppermute(first, "strip", [(j, i) for i, j in up])
    return before, after


def halo(shard):
    before, after = edges(shard[:1], shard[-1:])
    return [before, shard, after]


def with_edges(function, shards, borders):
    place = lax.axis_index("strip")
    inside = [place > 0, place < lax.axis_size("strip") - 1]
    sides = [
        jnp.where(there, function(*side), 0).astype(BF)
        for there, side in zip(inside, zip(*borders))
    ]
    return [sides[0], function(*shards), sides[1]]


def target_kernel(peaks_ref, count_ref, first_ref, gap_ref):
    gap_ref[...] = jnp.full(gap_ref.shape, FAR, jnp.float32)
    shape = gap_ref.shape[1:]
    row_ids = lax.broadcasted_iota(jnp.int32, shape, 0) + first_ref[0]
    col_ids = lax.broadcasted_iota(jnp.int32, shape, 1)

    def visit(slot, carry):
        row_gap = row_ids - peaks_ref[0, slot]
        col_gap = col_ids - peaks_ref[1, slot]
        distance = (row_gap * row_gap + col_gap * col_gap).astype(jnp.float32)
        kind = peaks_ref[2, slot]
        gap_ref[kind] = jnp.minimum(gap_ref[kind], distance)
        return carry

    lax.fori_loop(0, count_ref[0], visit, 0)


def nearest_gaps(box_peaks, box_count, first_row, row_total, col_total, classes):
    return pl.pallas_call(
        target_kernel,
        in_specs=[pl.BlockSpec(memory_space=pltpu.SMEM)] * 3,
        out_specs=pl.BlockSpec(memory_space=pltpu.VMEM),
        out_shape=jax.ShapeDtypeStruct((classes, row_total, col_total), jnp.float32),
        cost_estimate=SHORT,
        name="targets",
    )(box_peaks, box_count, first_row[None])


LANES = 128
SHORT = pl.CostEstimate(flops=1000, bytes_accessed=1000, transcendentals=0)
BF = jnp.bfloat16
F32 = jnp.float32


def plan(pixels, strips, strip_cells):
    per_strip = -(-strip_cells // LANES)
    high = strips * per_strip
    block = 352 if pixels % 352 == 0 and high <= 128 else 48
    return dict(
        per_strip=per_strip,
        high=high,
        offset=high // 2,
        block=block,
        stride=block + 4,
        group=block,
        strip_cells=strip_cells,
    )


def split_cells(index, plan):
    cell = index.astype(F32)
    strip = jnp.floor((cell + 0.5) * (1.0 / plan["strip_cells"]))
    rest = cell - strip * plan["strip_cells"]
    part = jnp.floor((rest + 0.5) * (1.0 / LANES))
    return strip * plan["per_strip"] + part - plan["offset"], rest - part * LANES


def softmax_lanes(logits, bins):
    lane = lax.broadcasted_iota(jnp.int32, logits.shape, 1)
    logits = jnp.where(lane < bins, logits, -jnp.inf)
    powers = jnp.exp(logits - jnp.max(logits, axis=1, keepdims=True))
    return powers / jnp.sum(powers, axis=1, keepdims=True)


def spread(ref, pixel, rows=16):
    return jnp.broadcast_to(ref[pl.ds(pixel, 1), :], (rows, LANES))


def one_hot(row, value, rows, offset=0):
    base = (lax.broadcasted_iota(jnp.int32, (rows, LANES), 0) - offset).astype(F32).astype(BF)
    none = jnp.zeros((16, LANES), BF)
    return [
        jnp.where(base[k : k + 16] == row, value, none) for k in range(0, rows, 16)
    ]


def high_pair(high_ref, depth_ref, first, plan):
    whole = plan["high"] // 16 * 16
    parts = []
    for j in range(2):
        row = spread(high_ref, first + j).astype(BF)
        value = spread(depth_ref, first + j).astype(BF)
        parts += one_hot(row, value, whole, plan["offset"])
    if whole < plan["high"]:
        both = [
            jnp.concatenate([spread(ref, first, 8), spread(ref, first + 1, 8)], 0).astype(BF)
            for ref in (high_ref, depth_ref)
        ]
        base = lax.broadcasted_iota(jnp.int32, (16, LANES), 0)
        base = jnp.where(base < 8, base, base - 8) + (whole - plan["offset"])
        none = jnp.zeros((16, LANES), BF)
        parts.append(jnp.where(base.astype(F32).astype(BF) == both[0], both[1], none))
    return jnp.concatenate(parts, 0)


def pool_kernel(place_ref, feat_ref, index_ref, weight_ref, own_ref, other_ref, dense_ref, both_ref, high_ref, low_ref, depth_ref, held, total, *, plan):
    bins = index_ref.shape[1]
    block, stride, high = (plan[k] for k in ("block", "stride", "high"))
    step = pl.program_id(0)

    @pl.when(step == 0)
    def _():
        high_ref[...] = jnp.zeros_like(high_ref)
        low_ref[...] = jnp.zeros_like(low_ref)
        total[...] = jnp.zeros_like(total)
        channels = total.shape[1]
        both_ref[...] = jnp.zeros_like(both_ref)
        both_ref[:bins] = weight_ref[:bins].astype(BF)
        both_ref[LANES : LANES + channels] = weight_ref[bins : bins + channels].astype(BF)

    feat = feat_ref[...]
    logits = lax.dot_general(feat, both_ref[:LANES], (((1,), (1,)), ((), ())), preferred_element_type=F32)
    depth_ref[...] = softmax_lanes(logits, bins)
    channels = total.shape[1]
    context_low = both_ref[LANES : LANES + channels]
    context = lax.dot_general(context_low, feat, (((1,), (1,)), ((), ())), preferred_element_type=F32).astype(BF)
    high_id, low_id = split_cells(index_ref[...], plan)
    high_ref[:, :bins] = high_id
    low_ref[:, :bins] = low_id
    one = jnp.ones((16, LANES), BF)

    def scatter(group, carry):
        for k in range(0, plan["group"], 2):
            first = group * plan["group"] + k
            left = high_pair(high_ref, depth_ref, first, plan)
            right = []
            for j in range(2):
                low = spread(low_ref, first + j).astype(BF)
                right.append(jnp.concatenate(one_hot(low, one, LANES), 0))
            tile = lax.dot_general(
                left, jnp.concatenate(right, 0), (((1,), (1,)), ((), ())), preferred_element_type=F32
            )
            whole = high // 16 * 16
            for j in range(2):
                part = tile[:, j * LANES : (j + 1) * LANES]
                held[pl.ds(first + j, whole, stride=stride), :] = part[j * whole : (j + 1) * whole]
                if whole < high:
                    held[pl.ds(first + j + whole * stride, 8, stride=stride), :] = part[
                        2 * whole + 8 * j : 2 * whole + 8 * j + 8
                    ]
        return carry

    lax.fori_loop(0, block // plan["group"], scatter, 0)

    def gather(k, carry):
        parts = []
        for j in range(2):
            part = held[pl.ds((k * 2 + j) * stride, block), :].astype(BF)
            dense_ref[k * 2 + j] = part
            parts.append(part)
        out = jnp.dot(context, jnp.concatenate(parts, 1), preferred_element_type=F32)
        for j in range(2):
            total[k * 2 + j] += out[:, j * LANES : (j + 1) * LANES]
        return carry

    lax.fori_loop(0, high // 2, gather, 0, unroll=36)

    @pl.when(step == pl.num_programs(0) - 1)
    def _():
        count = plan["per_strip"]
        chips = own_ref.shape[0]
        for shift in range(chips):
            chip = lax.rem(place_ref[0] + shift, chips)
            for ref, core in ((own_ref, place_ref[1]), (other_ref, 1 - place_ref[1])):
                first = (2 * chip + core) * count
                ref[shift] = total[pl.ds(first, count)].astype(BF)


def pool(place, features, index, weight, plan):
    pixels, width = features.shape
    bins = index.shape[1]
    channels = weight.shape[0] - bins
    block, high = plan["block"], plan["high"]
    halves = (high // plan["per_strip"] // 2, plan["per_strip"], channels, LANES)
    return pl.pallas_call(
        functools.partial(pool_kernel, plan=plan),
        grid=(pixels // block,),
        in_specs=[
            pl.BlockSpec(memory_space=pltpu.SMEM),
            pl.BlockSpec((block, width), lambda i: (i, 0)),
            pl.BlockSpec((block, bins), lambda i: (i, 0)),
            pl.BlockSpec(weight.shape, lambda i: (0, 0)),
        ],
        out_specs=[
            pl.BlockSpec(halves, lambda i: (0, 0, 0, 0)),
            pl.BlockSpec(halves, lambda i: (0, 0, 0, 0)),
            pl.BlockSpec((high, block, LANES), lambda i: (0, i, 0)),
            pl.BlockSpec((2 * LANES, width), lambda i: (0, 0)),
        ],
        out_shape=[
            jax.ShapeDtypeStruct(halves, BF),
            jax.ShapeDtypeStruct(halves, BF),
            jax.ShapeDtypeStruct((high, pixels, LANES), BF),
            jax.ShapeDtypeStruct((2 * LANES, width), BF),
        ],
        scratch_shapes=[pltpu.VMEM((block, LANES), F32)] * 3
        + [
            pltpu.VMEM((high * plan["stride"], LANES), F32),
            pltpu.VMEM((high, channels, LANES), F32),
        ],
        compiler_params=pltpu.CompilerParams(vmem_limit_bytes=40 << 20),
        cost_estimate=pl.CostEstimate(
            flops=4 * pixels * high * LANES * LANES,
            bytes_accessed=2 * pixels * high * LANES,
            transcendentals=0,
        ),
        name="pool",
    )(place, features, index, weight)


def unpool_kernel(place_ref, feat_ref, index_ref, both_ref, dense_ref, mine_ref, theirs_ref, head_ref, out_ref, high_ref, low_ref, pick_ref, held, sum_ref, grid_ref, grad_ref, *, plan):
    bins = index_ref.shape[1]
    channels = grid_ref.shape[1]
    chips, count = mine_ref.shape[:2]
    block, stride, high = (plan[k] for k in ("block", "stride", "high"))
    step = pl.program_id(0)

    @pl.when(step == 0)
    def _():
        high_ref[...] = jnp.zeros_like(high_ref)
        low_ref[...] = jnp.zeros_like(low_ref)
        held[...] = jnp.zeros_like(held)
        grad_ref[...] = jnp.zeros_like(grad_ref)
        for shift in range(chips):
            chip = lax.rem(place_ref[0] + (chips - shift), chips)
            for ref, core in ((mine_ref, place_ref[1]), (theirs_ref, 1 - place_ref[1])):
                grid_ref[pl.ds((2 * chip + core) * count, count)] = ref[shift]

    feat = feat_ref[...]
    logits = lax.dot_general(feat, both_ref[...], (((1,), (1,)), ((), ())), preferred_element_type=F32)
    depth = softmax_lanes(logits[:, :LANES], bins)
    context = logits[:, LANES : LANES + channels].astype(BF)
    high_id, low_id = split_cells(index_ref[...], plan)
    high_ref[:, :bins] = high_id
    low_ref[:, :bins] = low_id

    def project(k, carry):
        grid = jnp.concatenate([grid_ref[k * 2], grid_ref[k * 2 + 1]], 1)
        out = jnp.dot(context, grid, preferred_element_type=F32)
        for j in range(2):
            held[pl.ds((k * 2 + j) * stride, block), :] = out[:, j * LANES : (j + 1) * LANES]
        return carry

    lax.fori_loop(0, high // 2, project, 0, unroll=36)
    parts = 72

    def mix(k, carry):
        dense = jnp.concatenate([dense_ref[k * parts + j] for j in range(parts)], 1)
        grid = jnp.concatenate([grid_ref[k * parts + j] for j in range(parts)], 1)
        sum_ref[...] += lax.dot_general(
            dense, grid, (((1,), (1,)), ((), ())), preferred_element_type=F32
        )
        return carry

    sum_ref[...] = jnp.zeros_like(sum_ref)
    lax.fori_loop(0, high // parts, mix, 0)
    one = jnp.ones((16, LANES), BF)
    rows = (lax.broadcasted_iota(jnp.int32, (high, LANES), 0) - plan["offset"]).astype(F32)

    def collect(group, carry):
        for k in range(0, plan["group"], 2):
            first = group * plan["group"] + k
            left, right = [], []
            for j in range(2):
                left.append(held[pl.ds(first + j, high, stride=stride), :])
                low = spread(low_ref, first + j).astype(BF)
                right.append(jnp.concatenate(one_hot(low, one, LANES), 0))
            tile = jnp.dot(jnp.concatenate(left, 0).astype(BF), jnp.concatenate(right, 1), preferred_element_type=F32)
            for j in range(2):
                part = tile[j * high : (j + 1) * high, j * LANES : (j + 1) * LANES]
                kept = jnp.where(rows == high_ref[pl.ds(first + j, 1), :], part, 0.0)
                pick_ref[pl.ds(first + j, 1), :] = jnp.sum(kept, axis=0, keepdims=True)
        return carry

    lax.fori_loop(0, block // plan["group"], collect, 0)
    grad_prob = pick_ref[...]
    grad_context = sum_ref[...]
    grad_depth = depth * (grad_prob - jnp.sum(grad_prob * depth, axis=1, keepdims=True))
    grad_low = jnp.concatenate(
        [grad_depth, grad_context, jnp.zeros((block, LANES - channels), F32)], axis=1
    ).astype(BF)
    grad_ref[...] += lax.dot_general(grad_low, feat, (((0,), (0,)), ((), ())), preferred_element_type=F32)

    @pl.when(step == pl.num_programs(0) - 1)
    def _():
        first = LANES + channels
        rows = head_ref.shape[0]
        out_ref[:first] = grad_ref[:first].astype(BF)
        spare = jnp.zeros((2 * LANES - first - rows, grad_ref.shape[1]), F32)
        out_ref[first:] = jnp.concatenate([head_ref[...], spare], 0).astype(BF)


def unpool(place, features, index, both_low, dense, mine, theirs, head, plan):
    pixels, width = features.shape
    bins = index.shape[1]
    channels = mine.shape[2]
    block, high = plan["block"], plan["high"]
    return pl.pallas_call(
        functools.partial(unpool_kernel, plan=plan),
        grid=(pixels // block,),
        in_specs=[
            pl.BlockSpec(memory_space=pltpu.SMEM),
            pl.BlockSpec((block, width), lambda i: (i, 0)),
            pl.BlockSpec((block, bins), lambda i: (i, 0)),
            pl.BlockSpec(both_low.shape, lambda i: (0, 0)),
            pl.BlockSpec((high, block, LANES), lambda i: (0, i, 0)),
            pl.BlockSpec(mine.shape, lambda i: (0, 0, 0, 0)),
            pl.BlockSpec(theirs.shape, lambda i: (0, 0, 0, 0)),
            pl.BlockSpec(head.shape, lambda i: (0, 0)),
        ],
        out_specs=pl.BlockSpec((2 * LANES, width), lambda i: (0, 0)),
        out_shape=jax.ShapeDtypeStruct((2 * LANES, width), BF),
        scratch_shapes=[pltpu.VMEM((block, LANES), F32)] * 3
        + [
            pltpu.VMEM((high * plan["stride"], LANES), F32),
            pltpu.VMEM((block, channels), F32),
            pltpu.VMEM((high, channels, LANES), BF),
            pltpu.VMEM((2 * LANES, width), F32),
        ],
        compiler_params=pltpu.CompilerParams(vmem_limit_bytes=40 << 20),
        cost_estimate=pl.CostEstimate(
            flops=6 * pixels * high * LANES * LANES,
            bytes_accessed=2 * pixels * high * LANES,
            transcendentals=0,
        ),
        name="unpool",
    )(place, features, index, both_low, dense, mine, theirs, head)


def fill_windows(window_ref, part, cols, span):
    before_ref, shard_ref, after_ref = part
    rows = shard_ref.shape[0]
    width = window_ref.shape[2]
    window_ref[...] = jnp.zeros_like(window_ref)
    for row in range(rows + 2):
        if row == 0:
            line = before_ref[0]
        elif row == rows + 1:
            line = after_ref[0]
        else:
            line = shard_ref[row - 1]
        line = line[:, :width]
        start = row * span
        window_ref[0, start + 1 : start + cols] = line[: cols - 1]
        window_ref[1, start : start + cols] = line
        window_ref[2, start : start + cols - 1] = line[1:]


def window_scratch(part, width, span):
    return pltpu.VMEM((3, (part[1].shape[0] + 2) * span, width), BF)


def span_of(cols):
    return -(-cols // 16) * 16


def conv_kernel(*refs, count, turned, finish):
    kernels = refs[:count]
    parts = [refs[count + 3 * k : count + 3 * k + 3] for k in range(count)]
    rows, cols = parts[0][1].shape[:2]
    span = span_of(cols)
    windows = refs[-count:]
    left, right = [], []
    for part, window_ref, kernel_ref in zip(parts, windows, kernels):
        fill_windows(window_ref, part, cols, span)
        for tap in range(9):
            upward, across = tap // 3, tap % 3
            left.append(window_ref[across, upward * span : (upward + rows) * span])
            right.append(kernel_ref[8 - tap if turned else tap])
    left = jnp.concatenate(left, 1)
    if turned:
        total = jnp.dot(left, jnp.concatenate(right, 0), preferred_element_type=F32)
    else:
        total = lax.dot_general(
            left, jnp.concatenate(right, 1), (((1,), (1,)), ((), ())), preferred_element_type=F32
        )
    finish(total, rows, cols, span, *refs[4 * count : -count])


def keep_rows(total, rows, cols, span, out_ref):
    for row in range(rows):
        out_ref[row] = total[row * span : row * span + cols]


def keep_moments(total, rows, cols, span, *refs):
    out_ref, stats_ref = refs[-2:]
    keep_rows(total, rows, cols, span, out_ref)
    cells = float(rows * cols)
    center = jnp.sum(total, axis=0, keepdims=True) / cells
    spot = lax.broadcasted_iota(jnp.int32, (span, total.shape[1]), 0)
    spread_sum = jnp.zeros_like(center)
    for row in range(rows):
        apart = total[row * span : (row + 1) * span] - center
        apart = jnp.where(spot < cols, apart, 0.0)
        spread_sum = spread_sum + jnp.sum(apart * apart, axis=0, keepdims=True)
    hits = jnp.zeros_like(center)
    for ref in refs[:-2]:
        hits = jnp.full(center.shape, jnp.sum(jnp.where(ref[...] == 0.0, 1.0, 0.0)))
    stats = jnp.concatenate([center, spread_sum, hits], 0)

    def store(device, carry):
        stats_ref[device] = stats
        return carry

    lax.fori_loop(0, stats_ref.shape[0], store, 0)


def keep_grad(total, rows, cols, span, more_ref, norm_in_ref, vector_ref, out_ref, sums_ref):
    center, scale, gain, shift = (vector_ref[k : k + 1] for k in range(4))
    shift_sum = jnp.zeros_like(center)
    gain_sum = jnp.zeros_like(center)
    for row in range(rows):
        normed = (norm_in_ref[row] - center) * scale
        value = normed * gain + shift
        sig = jax.nn.sigmoid(value)
        grad = total[row * span : row * span + cols] + more_ref[row]
        grad = grad * (sig * (1.0 + value * (1.0 - sig)))
        out_ref[row] = grad
        shift_sum = shift_sum + jnp.sum(grad, axis=0, keepdims=True)
        gain_sum = gain_sum + jnp.sum(grad * normed, axis=0, keepdims=True)
    sums = jnp.concatenate([shift_sum, gain_sum], 0)

    def store(device, carry):
        sums_ref[device] = sums
        return carry

    lax.fori_loop(0, sums_ref.shape[0], store, 0)


def head_kernel(vector_ref, res_ref, act_ref, head_ref, bias_ref, gap_ref, count_ref, grad_ref, sums_ref, loss_ref, head_grad_ref):
    rows, cols, width = res_ref.shape
    center, scale, gain, shift = (vector_ref[k : k + 1] for k in range(4))
    head = head_ref[...]
    shift_sum = jnp.zeros_like(center)
    gain_sum = jnp.zeros_like(center)
    head_grad = jnp.zeros(head.shape, F32)
    bias_grad = jnp.zeros((head.shape[0], 1), F32)
    loss = jnp.zeros((head.shape[0], 1), F32)
    for row in range(rows):
        normed = (res_ref[row] - center) * scale
        summed = normed * gain + shift + act_ref[row].astype(F32)
        sig = jax.nn.sigmoid(summed)
        hidden = (summed * sig).astype(BF)
        logits = lax.dot_general(head, hidden, (((1,), (1,)), ((), ())), preferred_element_type=F32)
        logits = logits + bias_ref[...]
        prob = jax.nn.sigmoid(logits)
        tail = jnp.log1p(jnp.exp(-jnp.abs(logits)))
        soft_pos = jnp.maximum(logits, 0.0) + tail
        soft_neg = jnp.maximum(-logits, 0.0) + tail
        gap = gap_ref[:, row, :]
        heatmap = jnp.where(gap < FAR, jnp.exp(-gap / SPREAD_TWICE), 0.0)
        struck = jnp.where(gap == 0.0, 1.0, 0.0)
        weighting = (1.0 - heatmap) * (1.0 - heatmap)
        weighting = weighting * weighting
        miss = 1.0 - prob
        loss_here = struck * miss * miss * soft_neg + weighting * prob * prob * soft_pos
        loss = loss + jnp.sum(loss_here, axis=1, keepdims=True)
        grad_pos = -2.0 * prob * miss * miss * soft_neg - miss * miss * miss
        grad_neg = 2.0 * prob * prob * miss * soft_pos + prob * prob * prob
        grad_logits = (struck * grad_pos + weighting * grad_neg) / count_ref[...]
        grad_logits = grad_logits.astype(BF)
        bias_grad = bias_grad + jnp.sum(grad_logits.astype(F32), axis=1, keepdims=True)
        head_grad = head_grad + jnp.dot(grad_logits, hidden, preferred_element_type=F32)
        grad = lax.dot_general(grad_logits, head, (((0,), (0,)), ((), ())), preferred_element_type=F32)
        grad = grad * (sig * (1.0 + summed * (1.0 - sig)))
        grad_ref[row] = grad
        shift_sum = shift_sum + jnp.sum(grad, axis=0, keepdims=True)
        gain_sum = gain_sum + jnp.sum(grad * normed, axis=0, keepdims=True)
    loss_ref[...] = jnp.sum(loss, axis=0, keepdims=True)
    classes = head.shape[0]
    head_grad_ref[:classes] = head_grad
    down = lax.broadcasted_iota(jnp.int32, head.shape, 0)
    across = lax.broadcasted_iota(jnp.int32, head.shape, 1)
    bias_row = jnp.sum(jnp.where(down == across, bias_grad, 0.0), axis=0, keepdims=True)
    head_grad_ref[classes : classes + 1] = bias_row
    sums = jnp.concatenate([shift_sum, gain_sum], 0)

    def store(device, carry):
        sums_ref[device] = sums
        return carry

    lax.fori_loop(0, sums_ref.shape[0], store, 0)


def run_head(vectors, res_out, act, head_low, bias, gaps, positives, devices):
    rows, cols, width = res_out.shape
    classes = head_low.shape[0]
    shapes = [
        (rows, cols, width),
        (devices, 2, width),
        (1, 1),
        (classes + 1, width),
    ]
    return pl.pallas_call(
        head_kernel,
        in_specs=[pl.BlockSpec(memory_space=pltpu.VMEM)] * 7,
        out_specs=[pl.BlockSpec(memory_space=pltpu.VMEM)] * 4,
        out_shape=[jax.ShapeDtypeStruct(shape, F32) for shape in shapes],
        compiler_params=pltpu.CompilerParams(vmem_limit_bytes=24 << 20),
        name="head",
    )(vectors, res_out, act, head_low, bias, gaps, positives)


def keep_cells(total, rows, cols, span, out_ref):
    cells, channels = out_ref.shape[0] * LANES, out_ref.shape[1]
    flat = [total[row * span : row * span + cols] for row in range(rows)]
    flat.append(jnp.zeros((cells - rows * cols, total.shape[1]), F32))
    flat = jnp.concatenate(flat, 0)
    for part in range(out_ref.shape[0]):
        out_ref[part] = flat[part * LANES : (part + 1) * LANES].T[:channels].astype(BF)


def convolve(parts, kernels, turned, finish, outs, extras=()):
    rows, cols = parts[0][1].shape[:2]
    span = span_of(cols)
    widths = [kernel.shape[1] if turned else kernel.shape[2] for kernel in kernels]
    flat = [array for part in parts for array in part]
    operands = [*kernels, *flat, *extras]
    return pl.pallas_call(
        functools.partial(conv_kernel, count=len(parts), turned=turned, finish=finish),
        in_specs=[pl.BlockSpec(memory_space=pltpu.VMEM)] * len(operands),
        out_specs=[pl.BlockSpec(memory_space=pltpu.VMEM)] * len(outs),
        out_shape=outs,
        scratch_shapes=[
            window_scratch(part, width, span) for part, width in zip(parts, widths)
        ],
        compiler_params=pltpu.CompilerParams(vmem_limit_bytes=32 << 20),
        cost_estimate=pl.CostEstimate(
            flops=18 * rows * span * sum(widths) * kernels[0].shape[1],
            bytes_accessed=2 * sum(kernel.size for kernel in kernels),
            transcendentals=0,
        ),
        name="convolve",
    )(*operands)


def taps_kernel(place_ref, grad_ref, *refs, widths):
    count = len(widths)
    parts = [refs[3 * k : 3 * k + 3] for k in range(count)]
    own_ref, other_ref = refs[3 * count : 3 * count + 2]
    windows = refs[3 * count + 2 : 4 * count + 2]
    flipped_grad, total = refs[4 * count + 2 :]
    rows, cols, depth = grad_ref.shape
    owned = own_ref.shape[2]
    chips = own_ref.shape[0]
    span = span_of(cols)
    for part, window_ref in zip(parts, windows):
        fill_windows(window_ref, part, cols, span)
    flat = []
    for row in range(rows):
        flat += [grad_ref[row], jnp.zeros((span - cols, depth), BF)]
    flipped_grad[...] = jnp.concatenate(flat, 0).T

    def visit(tap, carry):
        start = pl.multiple_of((tap // 3) * span, 16)
        across = lax.rem(tap, 3)
        first = 0
        for window_ref in windows:
            window = window_ref[across, pl.ds(start, rows * span)]
            total[:, first : first + window.shape[1]] = jnp.dot(
                flipped_grad[...], window, preferred_element_type=F32
            )
            first += window.shape[1]
        for shift in range(chips):
            chip = lax.rem(place_ref[0] + shift, chips)
            for ref, core in ((own_ref, place_ref[1]), (other_ref, 1 - place_ref[1])):
                half = pl.multiple_of((2 * chip + core) * owned, 8)
                ref[shift, tap] = total[pl.ds(half, owned)].astype(BF)
        return carry

    lax.fori_loop(0, 9, visit, 0)


def taps(place, parts, widths, grad, chips):
    rows, cols, depth = grad.shape
    channels = sum(widths)
    span = span_of(cols)
    flat = [array for part in parts for array in part]
    half = jax.ShapeDtypeStruct((chips, 9, depth // chips // 2, channels), BF)
    return pl.pallas_call(
        functools.partial(taps_kernel, widths=widths),
        in_specs=[pl.BlockSpec(memory_space=pltpu.SMEM)]
        + [pl.BlockSpec(memory_space=pltpu.VMEM)] * (1 + len(flat)),
        out_specs=[pl.BlockSpec(memory_space=pltpu.VMEM)] * 2,
        out_shape=[half, half],
        scratch_shapes=[window_scratch(part, width, span) for part, width in zip(parts, widths)]
        + [pltpu.VMEM((depth, rows * span), BF), pltpu.VMEM((depth, channels), F32)],
        compiler_params=pltpu.CompilerParams(vmem_limit_bytes=28 << 20),
        cost_estimate=SHORT,
        name="taps",
    )(place, grad, *flat)


def settle_kernel(*refs):
    out_ref = refs[-1]
    rows, cols = out_ref.shape[:2]
    total = refs[0][...].astype(F32)
    for ref in refs[1:-1]:
        total = total + ref[...].astype(F32)
    parts = total.shape[0]
    flat = jnp.concatenate([total[part].T for part in range(parts)], 0)
    spare = jnp.zeros((cols, out_ref.shape[2] - flat.shape[1]), F32)
    for row in range(rows):
        line = flat[row * cols : (row + 1) * cols]
        out_ref[row] = jnp.concatenate([line, spare], 1).astype(BF)


def settle(parts, rows, cols):
    return pl.pallas_call(
        settle_kernel,
        in_specs=[pl.BlockSpec(memory_space=pltpu.VMEM)] * len(parts),
        out_specs=pl.BlockSpec(memory_space=pltpu.VMEM),
        out_shape=jax.ShapeDtypeStruct((rows, cols, LANES), BF),
        compiler_params=pltpu.CompilerParams(vmem_limit_bytes=32 << 20),
        name="settle",
    )(*parts)


def split_bits(value):
    pieces = []
    for _ in range(3):
        piece = value.astype(BF).astype(F32)
        pieces.append(piece)
        value = value - piece
    return pieces


def join_kernel(mixed_ref, loss_ref, *refs, hidden_width):
    parts = refs[:-2]
    share_ref, out_ref = refs[-2:]
    total = parts[0][...].astype(F32)
    for part in parts[1:]:
        total = total + part[...].astype(F32)
    share_ref[...] = total.astype(BF)
    square = jnp.sum(total * total, axis=0, keepdims=True)
    scalars = [
        jnp.sum(square[:, hidden_width:], axis=1, keepdims=True),
        jnp.sum(square[:, :hidden_width], axis=1, keepdims=True),
        loss_ref[...],
    ]
    mixed = jnp.sum(mixed_ref[...].astype(F32), axis=0)
    shape = (mixed.shape[0], LANES)
    lane = lax.broadcasted_iota(jnp.int32, shape, 1)
    row = jnp.zeros(shape, F32)
    for k, scalar in enumerate(scalars):
        for j, piece in enumerate(split_bits(scalar)):
            row = jnp.where(lane == 3 * k + j, piece, row)
    block = jnp.concatenate([mixed, row], 1).astype(BF)

    def store(device, carry):
        out_ref[device] = block
        return carry

    lax.fori_loop(0, out_ref.shape[0], store, 0)


def join_shares(mixed, loss, parts, hidden_width):
    devices, rows, width = mixed.shape
    return pl.pallas_call(
        functools.partial(join_kernel, hidden_width=hidden_width),
        in_specs=[pl.BlockSpec(memory_space=pltpu.VMEM)] * (2 + len(parts)),
        out_specs=[pl.BlockSpec(memory_space=pltpu.VMEM)] * 2,
        out_shape=[
            jax.ShapeDtypeStruct(parts[0].shape, BF),
            jax.ShapeDtypeStruct((devices, rows, width + LANES), BF),
        ],
        compiler_params=pltpu.CompilerParams(vmem_limit_bytes=16 << 20),
        name="join_shares",
    )(mixed, loss.reshape(1, 1), *parts)


def stage_kernel(after_ref, *refs):
    count = (len(refs) - 1) // 2
    sems = refs[-1]
    copies = [
        pltpu.make_async_copy(refs[k], refs[count + k], sems.at[k]) for k in range(count)
    ]
    for copy in copies:
        copy.start()
    for copy in copies:
        copy.wait()


def stage(after, arrays):
    return pl.pallas_call(
        stage_kernel,
        in_specs=[pl.BlockSpec(memory_space=pltpu.VMEM)]
        + [pl.BlockSpec(memory_space=pl.ANY)] * len(arrays),
        out_specs=[pl.BlockSpec(memory_space=pltpu.VMEM)] * len(arrays),
        out_shape=[jax.ShapeDtypeStruct(array.shape, array.dtype) for array in arrays],
        scratch_shapes=[pltpu.SemaphoreType.DMA((len(arrays),))],
        compiler_params=pltpu.CompilerParams(vmem_limit_bytes=16 << 20),
        cost_estimate=SHORT,
        name="stage",
    )(after, *arrays)


def squares(tensor):
    rows = (tensor * tensor).reshape(-1, tensor.shape[-1])
    return jnp.sum(jnp.sum(rows, axis=0, keepdims=True), axis=1, keepdims=True)


def update_kernel(place_ref, shared_ref, norm_ref, count_ref, *refs, shapes, rates, pieces):
    pieces_refs, refs = refs[:pieces], refs[pieces:]
    states, outputs = refs[:18], refs[18:38]
    mixed_ref, taps_scratch, load_sem, store_sem = refs[38:42]
    held = refs[42:]
    loads = [
        pltpu.make_async_copy(state, buffer, load_sem.at[k])
        for k, (state, buffer) in enumerate(zip(states, held))
    ]
    for k in (3, 4, 5, 6, 7, 8, 0, 1, 2) + tuple(range(9, 18)):
        loads[k].start()
    share, width = shared_ref.shape[1], mixed_ref.shape[1]
    for device in range(shared_ref.shape[0]):
        mixed_ref[device * share : (device + 1) * share] = shared_ref[device, :, :width].astype(F32)
    depth_bins, cam_width, classes, hidden_width = shapes
    if pieces > 1:
        for shift, ref in enumerate(pieces_refs):
            taps_scratch[lax.rem(place_ref[2] + (pieces - shift), pieces)] = ref[...].astype(F32)
        taps_ref = taps_scratch[...].reshape(9, held[3].shape[1], taps_scratch.shape[2])
    else:
        taps_ref = pieces_refs[0][...]
    mixed = mixed_ref[...]
    column = LANES + cam_width
    edge = taps_ref.shape[2] - cam_width
    grads = [
        jnp.concatenate([mixed[:depth_bins], mixed[LANES:column]], 0),
        jnp.concatenate([taps_ref[:, :, edge:], taps_ref[:, :, hidden_width:edge]], 2),
        taps_ref[:, :, :hidden_width],
        mixed[column : column + classes],
        norm_ref[...],
        mixed[column + classes : column + classes + 1, :classes],
    ]
    sums = jnp.sum(shared_ref[:, :1, width:].astype(F32), axis=0)
    lane = lax.broadcasted_iota(jnp.int32, sums.shape, 1)
    squared = [None if k in (1, 2) else squares(grad) for k, grad in enumerate(grads)]
    squared[1] = jnp.sum(jnp.where(lane < 3, sums, 0.0), axis=1, keepdims=True)
    squared[2] = jnp.sum(jnp.where((lane >= 3) & (lane < 6), sums, 0.0), axis=1, keepdims=True)
    loss_sum = jnp.sum(jnp.where((lane >= 6) & (lane < 9), sums, 0.0), axis=1, keepdims=True)
    loss_ref, norms_ref = outputs[:2]
    loss_ref[...] = loss_sum / count_ref[...]
    stores = [
        pltpu.make_async_copy(buffer, output, store_sem.at[k])
        for k, (buffer, output) in enumerate(zip(held, outputs[2:]))
    ]
    norms = jnp.zeros((1, LANES), F32)
    spot = lax.broadcasted_iota(jnp.int32, norms.shape, 1)
    for k in (1, 2, 0, 3, 4, 5):
        grad = grads[k]
        size = jnp.sqrt(jnp.broadcast_to(squared[k], (1, LANES)))
        norms = jnp.where(spot == k, jnp.log(size), norms)
        factor = CLIP_NORM / jnp.maximum(size, CLIP_NORM)
        factor = factor[:, :1]
        group = range(3 * k, 3 * k + 3)
        for j in group:
            loads[j].wait()
        weight, first, second = (held[j][...] for j in group)
        results = adamw(weight, grad * factor, first, second, rates[k], STEP)
        for j, result in zip(group, results):
            held[j][...] = result
            stores[j].start()
    norms_ref[...] = norms
    for store in stores:
        store.wait()


def update(place, shared, pieces, norm, positives, states, shapes, rates):
    args = [place, shared, norm, positives.reshape(1, 1)] + pieces + states
    count = len(pieces)
    width = norm.shape[1]
    return pl.pallas_call(
        functools.partial(update_kernel, shapes=shapes, rates=rates, pieces=count),
        in_specs=[pl.BlockSpec(memory_space=pltpu.SMEM)]
        + [pl.BlockSpec(memory_space=pltpu.VMEM)] * (3 + count)
        + [pl.BlockSpec(memory_space=pl.ANY)] * 18,
        out_specs=[pl.BlockSpec(memory_space=pltpu.VMEM)] * 2
        + [pl.BlockSpec(memory_space=pl.ANY)] * 18,
        out_shape=[jax.ShapeDtypeStruct((1, 1), F32), jax.ShapeDtypeStruct((1, LANES), F32)]
        + [jax.ShapeDtypeStruct(state.shape, F32) for state in states],
        scratch_shapes=[
            pltpu.VMEM((2 * LANES, width), F32),
            pltpu.VMEM((count, *pieces[0].shape[-2:]), F32),
            pltpu.SemaphoreType.DMA((18,)),
            pltpu.SemaphoreType.DMA((18,)),
        ]
        + [pltpu.VMEM(state.shape, F32) for state in states],
        compiler_params=pltpu.CompilerParams(vmem_limit_bytes=60 << 20),
        name="update",
    )(*args)


def swapped(tensor):
    strips = lax.axis_size("strip")
    return lax.ppermute(tensor, "strip", [(i, i ^ 1) for i in range(strips)])


def halves_summed(own, other):
    return own.astype(F32) + swapped(other).astype(F32)


def moved(tensor, shift):
    strips = lax.axis_size("strip")
    return lax.ppermute(tensor, "strip", [(i, (i + 2 * shift) % strips) for i in range(strips)])


def far_first(chips):
    return sorted(range(1, chips), key=lambda shift: -min(shift, chips - shift))


def along_chips(tensor):
    chips = tensor.shape[0]
    arrived = {shift: moved(tensor[shift], shift) for shift in far_first(chips)}
    return [tensor[0]] + [arrived[shift] for shift in range(1, chips)]


def total_of(parts):
    total = parts[0].astype(F32)
    for part in parts[1:]:
        total = total + part.astype(F32)
    return total


def from_chips(tensor):
    chips = lax.axis_size("strip") // 2
    arrived = {shift: moved(tensor, shift) for shift in far_first(chips)}
    return [tensor] + [arrived[shift] for shift in range(1, chips)]


def arrange_kernel(place_ref, mine_ref, theirs_ref, *outs):
    chips, taps_total, owned = mine_ref.shape[:3]
    for chip in range(chips):
        shift = lax.rem(place_ref[0] + (chips - chip), chips)
        for core in range(2):
            start = (2 * chip + core) * owned

            def copy(ref):
                first = 0
                for out_ref in outs:
                    width = out_ref.shape[2]

                    def one(tap, carry, out_ref=out_ref, first=first, width=width):
                        out_ref[tap, start : start + owned] = ref[
                            shift, tap, :, first : first + width
                        ]
                        return carry

                    lax.fori_loop(0, taps_total, one, 0)
                    first += width

            pl.when(place_ref[1] == core)(functools.partial(copy, mine_ref))
            pl.when(place_ref[1] != core)(functools.partial(copy, theirs_ref))


def arrange(place, mine, theirs, widths):
    chips, taps_total, owned = mine.shape[:3]
    return pl.pallas_call(
        arrange_kernel,
        in_specs=[pl.BlockSpec(memory_space=pltpu.SMEM)]
        + [pl.BlockSpec(memory_space=pltpu.VMEM)] * 2,
        out_specs=[pl.BlockSpec(memory_space=pltpu.VMEM)] * len(widths),
        out_shape=[
            jax.ShapeDtypeStruct((taps_total, 2 * chips * owned, width), BF) for width in widths
        ],
        compiler_params=pltpu.CompilerParams(vmem_limit_bytes=32 << 20),
        cost_estimate=SHORT,
        name="arrange",
    )(place, mine, theirs)


def moments(stats, cells, border):
    shared = lax.all_to_all(stats, ("batch", "strip"), 0, 0)
    if border:
        shared, border = lax.optimization_barrier((shared, border))
    centers = shared[:, 0]
    total = jnp.mean(centers, axis=0)
    spread_mean = jnp.mean(shared[:, 1] / cells + (centers - total) ** 2, axis=0)
    return (total, lax.rsqrt(spread_mean + EPS_NORM), jnp.sum(shared[:, 2, 0]), border)


def over_batch(tensor, shift):
    count = lax.axis_size("batch")
    if shift == 0:
        return tensor
    return lax.ppermute(tensor, "batch", [(i, (i + shift) % count) for i in range(count)])


def adamw(weight, gradient, first, second, rate, step_value):
    first = 0.9 * first + 0.1 * gradient
    second = 0.999 * second + 0.001 * gradient * gradient
    fix_one = 1.0 / (1.0 - 0.9**step_value)
    fix_two = 1.0 / (1.0 - 0.999**step_value)
    update = first * fix_one / (jnp.sqrt(second * fix_two) + 1e-08) + 0.01 * weight
    return (weight - rate * update, first, second)


def shards(
    camera_features,
    lidar_bev,
    pool_index,
    box_peaks,
    box_count,
    w_depth,
    m_depth,
    v_depth,
    w_join,
    m_join,
    v_join,
    w_res,
    m_res,
    v_res,
    w_head,
    m_head,
    v_head,
    norm_params,
    m_norm,
    v_norm,
    head_bias,
    m_bias,
    v_bias,
):
    samples, row_local, col_total, lidar_width = lidar_bev.shape
    strips = lax.axis_size("strip")
    row_total = row_local * strips
    cell_total = float(samples * lax.axis_size("batch") * row_total * col_total)
    depth_bins = pool_index.shape[2]
    classes = w_head.shape[1]
    owned = w_join.shape[3]
    cam_width = w_depth.shape[1] - depth_bins
    first_row = lax.axis_index("strip") * row_local
    place = lax.axis_index("strip")
    place = jnp.stack([place // 2, place % 2, lax.axis_index("batch")]).astype(jnp.int32)
    hidden_width = w_res.shape[2]
    taps_low = jnp.concatenate(
        [
            jnp.swapaxes(part, 2, 3).reshape(9, owned, -1)
            for part in (w_res, w_join[:, :, cam_width:], w_join[:, :, :cam_width])
        ],
        axis=2,
    ).astype(BF)
    taps_low = jnp.pad(taps_low, ((0, 0), (0, 0), (0, LANES - cam_width)))
    if owned % 16 == 0:
        taps_mine = from_chips(taps_low)
    strip_cells = row_local * col_total
    layout = plan(camera_features.shape[1], strips, strip_cells)
    own, other, dense, both_low = pool(
        place, camera_features[0], pool_index[0], w_depth.T, layout
    )
    if owned % 16 == 0:
        other, taps_mine = lax.optimization_barrier((other, taps_mine))
    pooled_halves = halves_summed(own, other).astype(BF)
    pooled = along_chips(pooled_halves)
    widths = [hidden_width, lidar_width, LANES]
    if owned % 16 == 0:
        taps_mine = jnp.stack(taps_mine)
        taps_full = arrange(place, taps_mine, swapped(taps_mine), widths)
    else:
        gathered = lax.all_gather(taps_low, "strip", axis=1, tiled=True)
        taps_full = jnp.split(gathered, [hidden_width, hidden_width + lidar_width], axis=2)
    lidar_parts = halo(lidar_bev[0])
    gaps = nearest_gaps(
        box_peaks[0], box_count, first_row, row_local, col_total, classes
    )
    pooled, gaps, taps_full, lidar_parts = lax.optimization_barrier(
        (pooled, gaps, taps_full, lidar_parts)
    )
    wide_out = jax.ShapeDtypeStruct((row_local, col_total, hidden_width), F32)
    axes = ("batch", "strip")
    devices = lax.axis_size(axes)
    stats_out = jax.ShapeDtypeStruct((devices, 3, hidden_width), F32)
    camera_parts = halo(settle(pooled, row_local, col_total))
    join_out, stats = convolve(
        [lidar_parts, camera_parts],
        taps_full[1:],
        False,
        keep_moments,
        [wide_out, stats_out],
        [gaps],
    )
    cells = float(strip_cells)
    center_one, scale_one, positives, join_border = moments(
        stats, cells, edges(join_out[:1], join_out[-1:])
    )

    def norm_one(values):
        return (values - center_one) * scale_one

    def act_of(values):
        return jax.nn.silu(norm_one(values) * norm_params[0] + norm_params[1]).astype(BF)

    act_parts = with_edges(act_of, [join_out], [join_border])
    act_one = act_parts[1]
    res_out, stats = convolve(
        [act_parts], taps_full[:1], False, keep_moments, [wide_out, stats_out]
    )
    center_two, scale_two, unused_term, unused_border = moments(stats, cells, ())

    def norm_two(values):
        return (values - center_two) * scale_two

    vectors = jnp.stack([center_two, scale_two, norm_params[2], norm_params[3]])
    grad_summed, sums, local_loss, grad_head = run_head(
        vectors,
        res_out,
        act_one,
        w_head.T.astype(BF),
        head_bias[:, None],
        gaps,
        positives.reshape(1, 1),
        devices,
    )
    shared = lax.all_to_all(sums, axes, 0, 0)
    shift_two, gain_two = jnp.sum(shared, axis=0)

    def grad_res_of(grad, values):
        spare = grad - shift_two / cell_total - norm_two(values) * gain_two / cell_total
        return (norm_params[2] * scale_two * spare).astype(BF)

    res_parts = halo(grad_res_of(grad_summed, res_out))
    sums_out = jax.ShapeDtypeStruct((devices, 2, hidden_width), F32)
    vectors = jnp.stack([center_one, scale_one, norm_params[0], norm_params[1]])
    grad_pre, sums = convolve(
        [res_parts],
        taps_full[:1],
        True,
        keep_grad,
        [wide_out, sums_out],
        [grad_summed, join_out, vectors],
    )
    shared = lax.all_to_all(sums, axes, 0, 0)
    shift_one, gain_one = jnp.sum(shared, axis=0)

    def grad_join_of(grad, values):
        spare = grad - shift_one / cell_total - norm_one(values) * gain_one / cell_total
        return (norm_params[0] * scale_one * spare).astype(BF)

    join_parts = halo(grad_join_of(grad_pre, join_out))
    cells_out = jax.ShapeDtypeStruct((layout["per_strip"], cam_width, LANES), BF)
    (grad_cells,) = convolve(
        [join_parts], taps_full[2:], True, keep_cells, [cells_out]
    )
    grad_cells, join_late, res_late = lax.optimization_barrier(
        (grad_cells, join_parts[1], res_parts[1])
    )
    grid_parts = from_chips(grad_cells)
    own_join, other_join = taps(
        place,
        [lidar_parts, camera_parts],
        [lidar_width, cam_width],
        join_late,
        strips // 2,
    )
    own_res, other_res = taps(place, [act_parts], [hidden_width], res_late, strips // 2)
    grid_parts, own_join, other_join, own_res, other_res = lax.optimization_barrier(
        (grid_parts, own_join, other_join, own_res, other_res)
    )
    grid_mine = jnp.stack(grid_parts)
    grid_theirs = swapped(grid_mine)
    grads = jnp.concatenate(
        [halves_summed(own_res, other_res), halves_summed(own_join, other_join)], axis=-1
    )
    taps_parts = along_chips(grads.astype(BF))
    grad_both = unpool(
        place,
        camera_features[0],
        pool_index[0],
        both_low,
        dense,
        grid_mine,
        grid_theirs,
        grad_head,
        layout,
    )
    grad_both, taps_parts = lax.optimization_barrier((grad_both, taps_parts))
    members = lax.axis_size("batch")
    member = lax.axis_index("batch")
    quarters = total_of(taps_parts).astype(BF).reshape(members, -1, (hidden_width + lidar_width + cam_width))
    parts = [
        over_batch(lax.dynamic_index_in_dim(quarters, (member + s) % members, 0, False), s)
        for s in range(members)
    ]
    width = w_depth.shape[0]
    mixed = grad_both.reshape(devices, -1, width)
    mixed = lax.all_to_all(mixed, axes, 0, 0)
    share, shared = join_shares(mixed, local_loss, parts, hidden_width)
    shared = lax.all_to_all(shared, axes, 0, 0)
    pieces = [over_batch(share, s) for s in range(members)]
    if share.shape[0] % 8:
        order = (member - jnp.arange(members)) % members
        pieces = [jnp.take(jnp.stack(pieces), order, axis=0).reshape(9, owned, -1).astype(F32)]
    grad_norm = jnp.stack([gain_one, shift_one, gain_two, shift_two])
    rates = [
        0.5 * w_depth.shape[0] ** (-0.5),
        0.5 * (9 * w_join.shape[2]) ** (-0.5),
        0.5 * (9 * w_res.shape[2]) ** (-0.5),
        0.5 * w_head.shape[0] ** (-0.5),
        SMALL_RATE,
        SMALL_RATE,
    ]
    weights = [w_depth, w_join, w_res, w_head, norm_params, head_bias]
    firsts = [m_depth, m_join, m_res, m_head, m_norm, m_bias]
    seconds = [v_depth, v_join, v_res, v_head, v_norm, v_bias]
    views = [
        jnp.transpose,
        lambda state: jnp.swapaxes(state, 2, 3).reshape(9, owned, -1),
        lambda state: jnp.swapaxes(state, 2, 3).reshape(9, owned, -1),
        jnp.transpose,
        lambda state: state,
        lambda state: state[None],
    ]
    backs = [
        jnp.transpose,
        lambda state: jnp.swapaxes(state.reshape(3, 3, owned, -1), 2, 3),
        lambda state: jnp.swapaxes(state.reshape(3, 3, owned, -1), 2, 3),
        jnp.transpose,
        lambda state: state,
        lambda state: state[0],
    ]
    states = [
        view(state)
        for view, group in zip(views, zip(weights, firsts, seconds))
        for state in group
    ]
    loss, norms, *states = update(
        place,
        shared,
        pieces,
        grad_norm,
        positives,
        states,
        (depth_bins, cam_width, classes, hidden_width),
        rates,
    )
    result = [loss[0], norms[0, :6]]
    for k, state in enumerate(states):
        result.append(backs[k // 3](state))
    return tuple(result)


def solution(mesh):
    in_specs = (
        P("batch", "strip", None),
        P("batch", "strip", None, None),
        P("batch", "strip", None),
        P("batch", None, None),
        P("batch"),
        P(),
        P(),
        P(),
        P(None, None, None, "strip"),
        P(None, None, None, "strip"),
        P(None, None, None, "strip"),
        P(None, None, None, "strip"),
        P(None, None, None, "strip"),
        P(None, None, None, "strip"),
        P(),
        P(),
        P(),
        P(),
        P(),
        P(),
        P(),
        P(),
        P(),
    )
    out_specs = (
        P(),
        P(),
        P(),
        P(),
        P(),
        P(None, None, None, "strip"),
        P(None, None, None, "strip"),
        P(None, None, None, "strip"),
        P(None, None, None, "strip"),
        P(None, None, None, "strip"),
        P(None, None, None, "strip"),
        P(),
        P(),
        P(),
        P(),
        P(),
        P(),
        P(),
        P(),
        P(),
    )
    return jax.shard_map(shards, mesh=mesh, in_specs=in_specs, out_specs=out_specs, check_vma=False)
```

profile of v0, /device:TPU:0, one launch (start us, length us, event | category | flops | bytes accessed | tf_op | source)
XLA Modules:
  0.0 275.3 jit_solution(3241941004129202172)
XLA Ops:
  2.0 3.1 %collective-permute-start = (bf16[9,32,640]{2,1,0:T(8,128)(2,1)S(1)}, bf16[9,32,640]{2,1,0:T(8,128)(2,1)S(1)}, u32[]{:S(2)}, u32[]{:S(2)}) collective-permute-start(bf16[9,32,640]{2,1,0:T(8,128)(2,1)S(1)} %fusion.4), channel_id=1, source_target_pairs={{0,2},{1,3},{2,4},{3,5},{4,6},{5,7},{6,0},{7,1},{8,10},{9,11},{10,... | collective-permute-start | bytes 1105928 | tf_op jit(solution)/shard_map/ppermute | solution.py:846
  5.1 2.6 collective-permute-start.1
  9.0 2.8 %copy.47 = s32[1,2112,118]{2,1,0:T(8,128)S(1)} copy(s32[1,2112,118]{1,0,2:T(1,128)} %param.25) | data formatting | bytes 1993728 | tf_op args[2]
  12.0 35.3 %pool.1 = (bf16[4,9,80,128]{3,2,1,0:T(8,128)(2,1)S(1)}, bf16[4,9,80,128]{3,2,1,0:T(8,128)(2,1)S(1)}, bf16[72,2112,128]{2,1,0:T(8,128)(2,1)}, bf16[256,256]{1,0:T(8,128)(2,1)S(1)}) custom-call(s32[3]{0:T(128)S(1)} %pad_add_fusion.place_ref, bf16[2112,256]{1,0:T(8,128)(2,1)S(1)} %bitcast.157, s32[2112,118]{1,0:T(8,128)S(1)} %bitcast.150, f32[198,256]{1,0:T(8,128)S(1)} %bitcast.155), custom_call_target="tpu_custom_call" | custom-call | flops 9965666304 | bytes 38928384 | tf_op jit(solution)/shard_map/pool/pallas_call | solution.py:217
  51.6 2.8 %collective-permute-start.6 = (bf16[9,80,128]{2,1,0:T(8,128)(2,1)}, bf16[9,80,128]{2,1,0:T(8,128)(2,1)}, u32[]{:S(2)}, u32[]{:S(2)}) collective-permute-start(bf16[9,80,128]{2,1,0:T(8,128)(2,1)} %get-tuple-element.182), channel_id=1, source_target_pairs={{0,6},{1,7},{2,0},{3,1},{4,2},{5,3},{6,4},{7,5},{8,14},{9,15},{10,... | collective-permute-start | bytes 552968 | tf_op jit(solution)/shard_map/ppermute | solution.py:846
  55.1 2.1 collective-permute-start.8
  59.8 2.1 targets.1.refs_8_.gap_ref
  68.8 2.0 collective-permute-start.10
  72.2 5.1 %collective-permute-done.11.refs_7_.refs_5_ = bf16[1,180,128]{2,1,0:T(8,128)(2,1)S(1)} collective-permute-done((bf16[1,180,128]{2,1,0:T(8,128)(2,1)S(1)}, bf16[1,180,128]{2,1,0:T(8,128)(2,1)S(1)}, u32[]{:S(2)}, u32[]{:S(2)}) %collective-permute-start.11) | collective-permute-done | bytes 46112 | tf_op jit(solution)/shard_map/ppermute | solution.py:24
  78.7 4.4 %convolve.4 = (f32[6,180,256]{2,1,0:T(8,128)S(1)}, f32[32,3,256]{2,1,0:T(4,128)}) custom-call(bf16[9,256,256]{2,1,0:T(8,128)(2,1)S(1)} %copy-done.26, bf16[9,256,128]{2,1,0:T(8,128)(2,1)S(1)} %copy-done.30, bf16[1,180,256]{2,1,0:T(8,128)(2,1)} %collective-permute-done.8.refs_2_.refs_0_, bf16[6,180,256]{2,1,0:T(8,128)(2,1)S(1)} %bitcast.152, ...), custom_call_target="tpu_custom_call" | custom-call | flops 2038431744 | bytes 1769472 | tf_op jit(solution)/shard_map/convolve/pallas_call | solution.py:561
  83.1 5.4 %all-to-all-start = ((f32[32,3,256]{2,1,0:T(4,128)}), f32[32,3,256]{2,1,0:T(4,128)S(1)}, u32[]{:S(2)}, u32[]{:S(2)}) async-start(f32[32,3,256]{2,1,0:T(4,128)} %get-tuple-element.120), calls=%async_computation | async-start | bytes 262144 | tf_op jit(solution)/shard_map/all_to_all | solution.py:914
  88.5 2.2 collective-permute-start.12
  92.2 2.9 %collective-permute-done.13 = f32[1,180,256]{2,1,0:T(8,128)S(1)} collective-permute-done((f32[1,180,256]{2,1,0:T(8,128)S(1)}, f32[1,180,256]{2,1,0:T(8,128)S(1)}, u32[]{:S(2)}, u32[]{:S(2)}) %collective-permute-start.13) | collective-permute-done | bytes 184352 | tf_op jit(solution)/shard_map/ppermute | solution.py:24
  98.0 2.6 convolve.5
  100.6 6.8 %all-to-all-start.1 = ((f32[32,3,256]{2,1,0:T(4,128)}), f32[32,3,256]{2,1,0:T(4,128)S(1)}, u32[]{:S(2)}, u32[]{:S(2)}) async-start(f32[32,3,256]{2,1,0:T(4,128)} %get-tuple-element.126), calls=%async_computation.1 | async-start | bytes 262144 | tf_op jit(solution)/shard_map/all_to_all | solution.py:914
  108.3 7.3 %all-to-all-done.1 = f32[32,3,256]{2,1,0:T(4,128)S(1)} async-done(((f32[32,3,256]{2,1,0:T(4,128)}), f32[32,3,256]{2,1,0:T(4,128)S(1)}, u32[]{:S(2)}, u32[]{:S(2)}) %all-to-all-start.1) | async-done | bytes 98336 | tf_op jit(solution)/shard_map/all_to_all | solution.py:914
  115.8 3.1 %head.1 = (f32[6,180,256]{2,1,0:T(8,128)S(1)}, f32[32,2,256]{2,1,0:T(2,128)S(1)}, f32[1,1]{1,0:T(1,128)}, f32[11,256]{1,0:T(8,128)S(1)}) custom-call(f32[4,256]{1,0:T(4,128)S(1)} %pad_maximum_fusion.3.vector_ref, f32[6,180,256]{2,1,0:T(8,128)S(1)} %get-tuple-element.127.res_ref, bf16[6,180,256]{2,1,0:T(8,128)(2,1)S(1)} %multiply_convert_fusion.2.refs_2_.act_ref.refs_1_, ...), custom_call_target="tpu_custom_call" | custom-call | tf_op jit(solution)/shard_map/head/pallas_call | solution.py:536
  119.9 9.1 %all_to_all.30 = f32[32,2,256]{2,1,0:T(2,128)S(1)} all-to-all(f32[32,2,256]{2,1,0:T(2,128)S(1)} %get-tuple-element.129), channel_id=1, replica_groups=mesh['batch'=4,'strip'=8] {'batch','strip'}, dimensions={0} | all-to-all | bytes 131072 | tf_op jit(solution)/shard_map/all_to_all | solution.py:1054
  130.8 2.0 collective-permute-start.14
  136.1 2.1 convolve.6
  139.1 11.3 %all_to_all.31 = f32[32,2,256]{2,1,0:T(2,128)S(1)} all-to-all(f32[32,2,256]{2,1,0:T(2,128)S(1)} %get-tuple-element.131), channel_id=1, replica_groups=mesh['batch'=4,'strip'=8] {'batch','strip'}, dimensions={0} | all-to-all | bytes 131072 | tf_op jit(solution)/shard_map/all_to_all | solution.py:1072
  152.1 2.0 collective-permute-start.16
  159.2 3.0 %collective-permute-start.18 = (bf16[9,80,128]{2,1,0:T(8,128)(2,1)S(1)}, bf16[9,80,128]{2,1,0:T(8,128)(2,1)S(1)}, u32[]{:S(2)}, u32[]{:S(2)}) collective-permute-start(bf16[9,80,128]{2,1,0:T(8,128)(2,1)S(1)} %convolve.7), channel_id=1, source_target_pairs={{0,2},{1,3},{2,4},{3,5},{4,6},{5,7},{6,0},{7,1},{8,10},{9,11},{10,... | collective-permute-start | bytes 552968 | tf_op jit(solution)/shard_map/ppermute | solution.py:846
  165.0 5.3 %taps.3 = (bf16[4,9,32,256]{3,2,1,0:T(8,128)(2,1)S(1)}, bf16[4,9,32,256]{3,2,1,0:T(8,128)(2,1)}) custom-call(s32[3]{0:T(128)S(1)} %pad_add_fusion.place_ref, bf16[6,180,256]{2,1,0:T(8,128)(2,1)S(1)} %multiply_convert_fusion.1.refs_2_.grad_ref, bf16[1,180,256]{2,1,0:T(8,128)(2,1)S(1)} %copy-done.12, ...), custom_call_target="tpu_custom_call" | custom-call | flops 1000 | bytes 1000 | tf_op jit(solution)/shard_map/taps/pallas_call | solution.py:622
  170.3 7.0 %taps.2 = (bf16[4,9,32,336]{3,2,1,0:T(8,128)(2,1)S(1)}, bf16[4,9,32,336]{3,2,1,0:T(8,128)(2,1)S(1)}) custom-call(s32[3]{0:T(128)S(1)} %pad_add_fusion.place_ref, bf16[6,180,256]{2,1,0:T(8,128)(2,1)S(1)} %multiply_convert_fusion.refs_2_.grad_ref, bf16[1,180,256]{2,1,0:T(8,128)(2,1)} %collective-permute-done.8.refs_2_.refs_0_, ...), custom_call_target="tpu_custom_call" | custom-call | flops 1000 | bytes 1000 | tf_op jit(solution)/shard_map/taps/pallas_call | solution.py:622
  183.8 3.2 %collective-permute-start.24 = (bf16[9,32,592]{2,1,0:T(8,128)(2,1)S(1)}, bf16[9,32,592]{2,1,0:T(8,128)(2,1)S(1)}, u32[]{:S(2)}, u32[]{:S(2)}) collective-permute-start(bf16[9,32,592]{2,1,0:T(8,128)(2,1)S(1)} %get-tuple-element.178), channel_id=1, source_target_pairs={{0,2},{1,3},{2,4},{3,5},{4,6},{5,7},{6,0},{7,1},{8,10},{9,11},{10,... | collective-permute-start | bytes 1022984 | tf_op jit(solution)/shard_map/ppermute | solution.py:846
  189.5 50.6 %unpool.1 = bf16[256,256]{1,0:T(8,128)(2,1)} custom-call(s32[3]{0:T(128)S(1)} %pad_add_fusion.place_ref, bf16[2112,256]{1,0:T(8,128)(2,1)S(1)} %bitcast.158, s32[2112,118]{1,0:T(8,128)S(1)} %bitcast.151, bf16[256,256]{1,0:T(8,128)(2,1)S(1)} %copy-done.33, bf16[72,2112,128]{2,1,0:T(8,128)(2,1)} %get-tuple-element.99.dense_ref, ...), custom_call_target="tpu_custom_call" | custom-call | flops 14948499456 | bytes 38928384 | tf_op jit(solution)/shard_map/unpool/pallas_call | solution.py:340
  240.1 2.6 all-to-all-start.4
  247.6 2.7 collective-permute-done.27.refs_1_
  253.3 4.6 %all-to-all-start.5 = ((bf16[32,8,384]{2,1,0:T(8,128)(2,1)}), bf16[32,8,384]{2,1,0:T(8,128)(2,1)S(1)}, u32[]{:S(2)}, u32[]{:S(2)}) async-start(bf16[32,8,384]{2,1,0:T(8,128)(2,1)} %get-tuple-element.154), calls=%async_computation.5 | async-start | bytes 393216 | tf_op jit(solution)/shard_map/all_to_all | solution.py:1128
  263.3 2.4 collective-permute-done.30.refs_1_
  268.3 5.9 %update.1 = (f32[1,1]{1,0:T(1,128)}, f32[1,128]{1,0:T(1,128)}, f32[198,256]{1,0:T(8,128)}, f32[198,256]{1,0:T(8,128)}, f32[198,256]{1,0:T(8,128)}, /*index=5*/f3...) custom-call(s32[3]{0:T(128)} %copy-done.21, ...), custom_call_target="tpu_custom_call" | custom-call | tf_op jit(solution)/shard_map/update/pallas_call | solution.py:814
  (192 shorter events, 66.6 us)
Async XLA Ops:
  2.0 45.2 %collective-permute-start = (bf16[9,32,640]{2,1,0:T(8,128)(2,1)S(1)}, bf16[9,32,640]{2,1,0:T(8,128)(2,1)S(1)}, u32[]{:S(2)}, u32[]{:S(2)}) collective-permute-start(bf16[9,32,640]{2,1,0:T(8,128)(2,1)S(1)} %fusion.4), channel_id=1, source_target_pairs={{0,2},{1,3},{2,4},{3,5},{4,6},{5,7},{6,0},{7,1},{8,10},{9,11},{10,... | collective-permute-start | bytes 1105928 | tf_op jit(solution)/shard_map/ppermute | solution.py:846
  5.1 42.2 %collective-permute-start.1 = (bf16[9,32,640]{2,1,0:T(8,128)(2,1)S(1)}, bf16[9,32,640]{2,1,0:T(8,128)(2,1)S(1)}, u32[]{:S(2)}, u32[]{:S(2)}) collective-permute-start(bf16[9,32,640]{2,1,0:T(8,128)(2,1)S(1)} %fusion.4), channel_id=1, source_target_pairs={{0,4},{1,5},{2,6},{3,7},{4,0},{5,1},{6,2},{7,3},{8,12},{9,13},{10,... | collective-permute-start | bytes 1105928 | tf_op jit(solution)/shard_map/ppermute | solution.py:846
  7.7 39.6 %collective-permute-start.2 = (bf16[9,32,640]{2,1,0:T(8,128)(2,1)S(1)}, bf16[9,32,640]{2,1,0:T(8,128)(2,1)}, u32[]{:S(2)}, u32[]{:S(2)}) collective-permute-start(bf16[9,32,640]{2,1,0:T(8,128)(2,1)S(1)} %fusion.4), channel_id=1, source_target_pairs={{0,6},{1,7},{2,0},{3,1},{4,2},{5,3},{6,4},{7,5},{8,14},{9,15},{10,... | collective-permute-start | bytes 1105928 | tf_op jit(solution)/shard_map/ppermute | solution.py:846
  48.5 8.7 %collective-permute-start.7 = (bf16[4,9,32,640]{3,2,1,0:T(8,128)(2,1)S(1)}, bf16[4,9,32,640]{3,2,1,0:T(8,128)(2,1)S(1)}, u32[]{:S(2)}, u32[]{:S(2)}) collective-permute-start(bf16[4,9,32,640]{3,2,1,0:T(8,128)(2,1)S(1)} %pad_maximum_fusion.mine_ref), channel_id=1, source_target_pairs={{0,1},{1,0},{2,3},{3,2},{4,5},{5,4},{6,7},{7,6},{8,9},{9,8},{10,11... | collective-permute-start | bytes 4423688 | tf_op jit(solution)/shard_map/ppermute | solution.py:837
  50.6 15.1 %collective-permute-start.4 = (bf16[9,80,128]{2,1,0:T(8,128)(2,1)}, bf16[9,80,128]{2,1,0:T(8,128)(2,1)}, u32[]{:S(2)}, u32[]{:S(2)}) collective-permute-start(bf16[9,80,128]{2,1,0:T(8,128)(2,1)} %get-tuple-element.184), channel_id=1, source_target_pairs={{0,2},{1,3},{2,4},{3,5},{4,6},{5,7},{6,0},{7,1},{8,10},{9,11},{10,... | collective-permute-start | bytes 552968 | tf_op jit(solution)/shard_map/ppermute | solution.py:846
  51.3 16.2 %collective-permute-start.5 = (bf16[9,80,128]{2,1,0:T(8,128)(2,1)}, bf16[9,80,128]{2,1,0:T(8,128)(2,1)}, u32[]{:S(2)}, u32[]{:S(2)}) collective-permute-start(bf16[9,80,128]{2,1,0:T(8,128)(2,1)} %get-tuple-element.183), channel_id=1, source_target_pairs={{0,4},{1,5},{2,6},{3,7},{4,0},{5,1},{6,2},{7,3},{8,12},{9,13},{10,... | collective-permute-start | bytes 552968 | tf_op jit(solution)/shard_map/ppermute | solution.py:846
  51.6 15.9 %collective-permute-start.6 = (bf16[9,80,128]{2,1,0:T(8,128)(2,1)}, bf16[9,80,128]{2,1,0:T(8,128)(2,1)}, u32[]{:S(2)}, u32[]{:S(2)}) collective-permute-start(bf16[9,80,128]{2,1,0:T(8,128)(2,1)} %get-tuple-element.182), channel_id=1, source_target_pairs={{0,6},{1,7},{2,0},{3,1},{4,2},{5,3},{6,4},{7,5},{8,14},{9,15},{10,... | collective-permute-start | bytes 552968 | tf_op jit(solution)/shard_map/ppermute | solution.py:846
  55.1 10.5 %collective-permute-start.8 = (bf16[1,180,256]{2,1,0:T(8,128)(2,1)}, bf16[1,180,256]{2,1,0:T(8,128)(2,1)}, u32[]{:S(2)}, u32[]{:S(2)}) collective-permute-start(bf16[1,180,256]{2,1,0:T(8,128)(2,1)} %get-tuple-element.191), channel_id=1, source_target_pairs={{0,1},{1,2},{2,3},{3,4},{4,5},{5,6},{6,7},{8,9},{9,10},{10,11},{11... | collective-permute-start | bytes 276488 | tf_op jit(solution)/shard_map/ppermute | solution.py:23
  57.2 8.4 %collective-permute-start.9 = (bf16[1,180,256]{2,1,0:T(8,128)(2,1)}, bf16[1,180,256]{2,1,0:T(8,128)(2,1)}, u32[]{:S(2)}, u32[]{:S(2)}) collective-permute-start(bf16[1,180,256]{2,1,0:T(8,128)(2,1)} %get-tuple-element.190), channel_id=1, source_target_pairs={{1,0},{2,1},{3,2},{4,3},{5,4},{6,5},{7,6},{9,8},{10,9},{11,10},{12... | collective-permute-start | bytes 276488 | tf_op jit(solution)/shard_map/ppermute | solution.py:24
  68.8 3.4 %collective-permute-start.10 = (bf16[1,180,128]{2,1,0:T(8,128)(2,1)S(1)}, bf16[1,180,128]{2,1,0:T(8,128)(2,1)S(1)}, u32[]{:S(2)}, u32[]{:S(2)}) collective-permute-start(bf16[1,180,128]{2,1,0:T(8,128)(2,1)S(1)} %get-tuple-element.197), channel_id=1, source_target_pairs={{0,1},{1,2},{2,3},{3,4},{4,5},{5,6},{6,7},{8,9},{9,10},{10,11},{11... | collective-permute-start | bytes 138248 | tf_op jit(solution)/shard_map/ppermute | solution.py:23
  70.9 6.5 %collective-permute-start.11 = (bf16[1,180,128]{2,1,0:T(8,128)(2,1)S(1)}, bf16[1,180,128]{2,1,0:T(8,128)(2,1)S(1)}, u32[]{:S(2)}, u32[]{:S(2)}) collective-permute-start(bf16[1,180,128]{2,1,0:T(8,128)(2,1)S(1)} %get-tuple-element.196), channel_id=1, source_target_pairs={{1,0},{2,1},{3,2},{4,3},{5,4},{6,5},{7,6},{9,8},{10,9},{11,10},{12... | collective-permute-start | bytes 138248 | tf_op jit(solution)/shard_map/ppermute | solution.py:24
  83.1 13.6 %all-to-all-start = ((f32[32,3,256]{2,1,0:T(4,128)}), f32[32,3,256]{2,1,0:T(4,128)S(1)}, u32[]{:S(2)}, u32[]{:S(2)}) async-start(f32[32,3,256]{2,1,0:T(4,128)} %get-tuple-element.120), calls=%async_computation | async-start | bytes 262144 | tf_op jit(solution)/shard_map/all_to_all | solution.py:914
  88.5 3.7 %collective-permute-start.12 = (f32[1,180,256]{2,1,0:T(8,128)S(1)}, f32[1,180,256]{2,1,0:T(8,128)S(1)}, u32[]{:S(2)}, u32[]{:S(2)}) collective-permute-start(f32[1,180,256]{2,1,0:T(8,128)S(1)} %get-tuple-element.181), channel_id=1, source_target_pairs={{0,1},{1,2},{2,3},{3,4},{4,5},{5,6},{6,7},{8,9},{9,10},{10,11},{11... | collective-permute-start | bytes 552968 | tf_op jit(solution)/shard_map/ppermute | solution.py:23
  90.7 4.5 %collective-permute-start.13 = (f32[1,180,256]{2,1,0:T(8,128)S(1)}, f32[1,180,256]{2,1,0:T(8,128)S(1)}, u32[]{:S(2)}, u32[]{:S(2)}) collective-permute-start(f32[1,180,256]{2,1,0:T(8,128)S(1)} %get-tuple-element.180), channel_id=1, source_target_pairs={{1,0},{2,1},{3,2},{4,3},{5,4},{6,5},{7,6},{9,8},{10,9},{11,10},{12... | collective-permute-start | bytes 552968 | tf_op jit(solution)/shard_map/ppermute | solution.py:24
  100.6 15.0 %all-to-all-start.1 = ((f32[32,3,256]{2,1,0:T(4,128)}), f32[32,3,256]{2,1,0:T(4,128)S(1)}, u32[]{:S(2)}, u32[]{:S(2)}) async-start(f32[32,3,256]{2,1,0:T(4,128)} %get-tuple-element.126), calls=%async_computation.1 | async-start | bytes 262144 | tf_op jit(solution)/shard_map/all_to_all | solution.py:914
  152.1 3.5 %collective-permute-start.16 = (bf16[1,180,256]{2,1,0:T(8,128)(2,1)S(1)}, bf16[1,180,256]{2,1,0:T(8,128)(2,1)S(1)}, u32[]{:S(2)}, u32[]{:S(2)}) collective-permute-start(bf16[1,180,256]{2,1,0:T(8,128)(2,1)S(1)} %get-tuple-element.187), channel_id=1, source_target_pairs={{0,1},{1,2},{2,3},{3,4},{4,5},{5,6},{6,7},{8,9},{9,10},{10,11},{11... | collective-permute-start | bytes 276488 | tf_op jit(solution)/shard_map/ppermute | solution.py:23
  159.2 18.2 %collective-permute-start.18 = (bf16[9,80,128]{2,1,0:T(8,128)(2,1)S(1)}, bf16[9,80,128]{2,1,0:T(8,128)(2,1)S(1)}, u32[]{:S(2)}, u32[]{:S(2)}) collective-permute-start(bf16[9,80,128]{2,1,0:T(8,128)(2,1)S(1)} %convolve.7), channel_id=1, source_target_pairs={{0,2},{1,3},{2,4},{3,5},{4,6},{5,7},{6,0},{7,1},{8,10},{9,11},{10,... | collective-permute-start | bytes 552968 | tf_op jit(solution)/shard_map/ppermute | solution.py:846
  162.2 15.1 %collective-permute-start.19 = (bf16[9,80,128]{2,1,0:T(8,128)(2,1)S(1)}, bf16[9,80,128]{2,1,0:T(8,128)(2,1)S(1)}, u32[]{:S(2)}, u32[]{:S(2)}) collective-permute-start(bf16[9,80,128]{2,1,0:T(8,128)(2,1)S(1)} %convolve.7), channel_id=1, source_target_pairs={{0,4},{1,5},{2,6},{3,7},{4,0},{5,1},{6,2},{7,3},{8,12},{9,13},{10,... | collective-permute-start | bytes 552968 | tf_op jit(solution)/shard_map/ppermute | solution.py:846
  163.1 14.3 %collective-permute-start.20 = (bf16[9,80,128]{2,1,0:T(8,128)(2,1)S(1)}, bf16[9,80,128]{2,1,0:T(8,128)(2,1)S(1)}, u32[]{:S(2)}, u32[]{:S(2)}) collective-permute-start(bf16[9,80,128]{2,1,0:T(8,128)(2,1)S(1)} %convolve.7), channel_id=1, source_target_pairs={{0,6},{1,7},{2,0},{3,1},{4,2},{5,3},{6,4},{7,5},{8,14},{9,15},{10,... | collective-permute-start | bytes 552968 | tf_op jit(solution)/shard_map/ppermute | solution.py:846
  178.1 4.1 %collective-permute-start.23 = (bf16[4,9,32,336]{3,2,1,0:T(8,128)(2,1)S(1)}, bf16[4,9,32,336]{3,2,1,0:T(8,128)(2,1)}, u32[]{:S(2)}, u32[]{:S(2)}) collective-permute-start(bf16[4,9,32,336]{3,2,1,0:T(8,128)(2,1)S(1)} %get-tuple-element.147), channel_id=1, source_target_pairs={{0,1},{1,0},{2,3},{3,2},{4,5},{5,4},{6,7},{7,6},{8,9},{9,8},{10,11... | collective-permute-start | bytes 2322440 | tf_op jit(solution)/shard_map/ppermute | solution.py:837
  178.3 11.2 %collective-permute-start.21 = (bf16[4,9,80,128]{3,2,1,0:T(8,128)(2,1)S(1)}, bf16[4,9,80,128]{3,2,1,0:T(8,128)(2,1)S(1)}, u32[]{:S(2)}, u32[]{:S(2)}) collective-permute-start(bf16[4,9,80,128]{3,2,1,0:T(8,128)(2,1)S(1)} %pad_maximum_fusion.1.mine_ref), channel_id=1, source_target_pairs={{0,1},{1,0},{2,3},{3,2},{4,5},{5,4},{6,7},{7,6},{8,9},{9,8},{10,11... | collective-permute-start | bytes 2211848 | tf_op jit(solution)/shard_map/ppermute | solution.py:837
  183.8 56.3 %collective-permute-start.24 = (bf16[9,32,592]{2,1,0:T(8,128)(2,1)S(1)}, bf16[9,32,592]{2,1,0:T(8,128)(2,1)S(1)}, u32[]{:S(2)}, u32[]{:S(2)}) collective-permute-start(bf16[9,32,592]{2,1,0:T(8,128)(2,1)S(1)} %get-tuple-element.178), channel_id=1, source_target_pairs={{0,2},{1,3},{2,4},{3,5},{4,6},{5,7},{6,0},{7,1},{8,10},{9,11},{10,... | collective-permute-start | bytes 1022984 | tf_op jit(solution)/shard_map/ppermute | solution.py:846
  187.0 53.1 %collective-permute-start.25 = (bf16[9,32,592]{2,1,0:T(8,128)(2,1)S(1)}, bf16[9,32,592]{2,1,0:T(8,128)(2,1)S(1)}, u32[]{:S(2)}, u32[]{:S(2)}) collective-permute-start(bf16[9,32,592]{2,1,0:T(8,128)(2,1)S(1)} %get-tuple-element.179), channel_id=1, source_target_pairs={{0,4},{1,5},{2,6},{3,7},{4,0},{5,1},{6,2},{7,3},{8,12},{9,13},{10,... | collective-permute-start | bytes 1022984 | tf_op jit(solution)/shard_map/ppermute | solution.py:846
  188.8 51.3 %collective-permute-start.26 = (bf16[9,32,592]{2,1,0:T(8,128)(2,1)S(1)}, bf16[9,32,592]{2,1,0:T(8,128)(2,1)S(1)}, u32[]{:S(2)}, u32[]{:S(2)}) collective-permute-start(bf16[9,32,592]{2,1,0:T(8,128)(2,1)S(1)} %get-tuple-element.176), channel_id=1, source_target_pairs={{0,6},{1,7},{2,0},{3,1},{4,2},{5,3},{6,4},{7,5},{8,14},{9,15},{10,... | collective-permute-start | bytes 1022984 | tf_op jit(solution)/shard_map/ppermute | solution.py:846
  240.1 11.6 %all-to-all-start.4 = ((bf16[32,8,256]{2,1,0:T(8,128)(2,1)}), bf16[32,8,256]{2,1,0:T(8,128)(2,1)S(1)}, u32[]{:S(2)}, u32[]{:S(2)}) async-start(bf16[32,8,256]{2,1,0:T(8,128)(2,1)} %bitcast.49), calls=%async_computation.4 | async-start | bytes 262144 | tf_op jit(solution)/shard_map/all_to_all | solution.py:1126
  243.0 7.3 %collective-permute-start.27 = (bf16[72,592]{1,0:T(8,128)(2,1)S(1)}, bf16[72,592]{1,0:T(8,128)(2,1)S(1)}, u32[]{:S(2)}, u32[]{:S(2)}) collective-permute-start(bf16[72,592]{1,0:T(8,128)(2,1)S(1)} %get-tuple-element.194), channel_id=1, source_target_pairs={{0,8},{8,16},{16,24},{24,0},{1,9},{9,17},{17,25},{25,1},{2,10},{10... | collective-permute-start | bytes 255752 | tf_op jit(solution)/shard_map/ppermute | solution.py:927
  244.6 7.0 %collective-permute-start.28 = (bf16[72,592]{1,0:T(8,128)(2,1)S(1)}, bf16[72,592]{1,0:T(8,128)(2,1)S(1)}, u32[]{:S(2)}, u32[]{:S(2)}) collective-permute-start(bf16[72,592]{1,0:T(8,128)(2,1)S(1)} %get-tuple-element.193), channel_id=1, source_target_pairs={{0,16},{8,24},{16,0},{24,8},{1,17},{9,25},{17,1},{25,9},{2,18},{10... | collective-permute-start | bytes 255752 | tf_op jit(solution)/shard_map/ppermute | solution.py:927
  246.1 5.5 %collective-permute-start.29 = (bf16[72,592]{1,0:T(8,128)(2,1)S(1)}, bf16[72,592]{1,0:T(8,128)(2,1)S(1)}, u32[]{:S(2)}, u32[]{:S(2)}) collective-permute-start(bf16[72,592]{1,0:T(8,128)(2,1)S(1)} %get-tuple-element.192), channel_id=1, source_target_pairs={{0,24},{8,0},{16,8},{24,16},{1,25},{9,1},{17,9},{25,17},{2,26},{10... | collective-permute-start | bytes 255752 | tf_op jit(solution)/shard_map/ppermute | solution.py:927
  253.3 14.2 %all-to-all-start.5 = ((bf16[32,8,384]{2,1,0:T(8,128)(2,1)}), bf16[32,8,384]{2,1,0:T(8,128)(2,1)S(1)}, u32[]{:S(2)}, u32[]{:S(2)}) async-start(bf16[32,8,384]{2,1,0:T(8,128)(2,1)} %get-tuple-element.154), calls=%async_computation.5 | async-start | bytes 393216 | tf_op jit(solution)/shard_map/all_to_all | solution.py:1128
  258.0 7.7 %collective-permute-start.30 = (bf16[72,592]{1,0:T(8,128)(2,1)S(1)}, bf16[72,592]{1,0:T(8,128)(2,1)S(1)}, u32[]{:S(2)}, u32[]{:S(2)}) collective-permute-start(bf16[72,592]{1,0:T(8,128)(2,1)S(1)} %get-tuple-element.155.refs_0_), channel_id=1, source_target_pairs={{0,8},{8,16},{16,24},{24,0},{1,9},{9,17},{17,25},{25,1},{2,10},{10... | collective-permute-start | bytes 255752 | tf_op jit(solution)/shard_map/ppermute | solution.py:927
  259.8 7.7 %collective-permute-start.31 = (bf16[72,592]{1,0:T(8,128)(2,1)S(1)}, bf16[72,592]{1,0:T(8,128)(2,1)S(1)}, u32[]{:S(2)}, u32[]{:S(2)}) collective-permute-start(bf16[72,592]{1,0:T(8,128)(2,1)S(1)} %get-tuple-element.155.refs_0_), channel_id=1, source_target_pairs={{0,16},{8,24},{16,0},{24,8},{1,17},{9,25},{17,1},{25,9},{2,18},{10... | collective-permute-start | bytes 255752 | tf_op jit(solution)/shard_map/ppermute | solution.py:927
  261.2 6.3 %collective-permute-start.32 = (bf16[72,592]{1,0:T(8,128)(2,1)S(1)}, bf16[72,592]{1,0:T(8,128)(2,1)S(1)}, u32[]{:S(2)}, u32[]{:S(2)}) collective-permute-start(bf16[72,592]{1,0:T(8,128)(2,1)S(1)} %get-tuple-element.155.refs_0_), channel_id=1, source_target_pairs={{0,24},{8,0},{16,8},{24,16},{1,25},{9,1},{17,9},{25,17},{2,26},{10... | collective-permute-start | bytes 255752 | tf_op jit(solution)/shard_map/ppermute | solution.py:927
  (48 other events, 504.8 us)
where the time goes:
time: 276 us; the launch traced here: 275 us
  Pallas kernels  125 us (45%)
  starting transfers between devices  70.1 us (25%)
  waiting for transfers between devices  33.2 us (12%)
  blocking collectives  20.4 us (7%)
  local copies, waits for them, and re-layouts  13.2 us (5%)
  other arithmetic  11.4 us (4%)
    pallas_call x1, Pallas kernels, unpool(): pl.pallas_call(functools.partial(unpool_kernel, plan=plan), grid=(pixels...  50.6 us
    pallas_call x1, Pallas kernels, pool(): pl.pallas_call(functools.partial(pool_kernel, plan=plan), grid=(pixels //...  35.3 us
    ppermute x12, starting transfers between devices, moved(): lax.ppermute(tensor, 'strip', [(i, (i + 2 * shift) % strips) for i in ran...  22.3 us
    all_to_all x2, blocking collectives, shards(): shared = lax.all_to_all(sums, axes, 0, 0)  20.4 us
    pallas_call x2, Pallas kernels, taps(): pl.pallas_call(functools.partial(taps_kernel, widths=widths), in_specs=[p...  12.3 us
    all_to_all x2, starting transfers between devices, moments(): shared = lax.all_to_all(stats, ('batch', 'strip'), 0, 0)  12.2 us
    ppermute x5, waiting for transfers between devices, edges(): after = lax.ppermute(first, 'strip', [(j, i) for i, j in up])  11.8 us
    pallas_call x4, Pallas kernels, convolve(): pl.pallas_call(functools.partial(conv_kernel, count=len(parts), turned=tu...  10.7 us
  transfers between devices with their start and end apart: 37, of which 14 were waited for; matrix products, arithmetic and copies ran while one was open for 4% of the time, Pallas kernels for 37%

commit v1 on v0

--- a/solution.py
+++ b/solution.py
@@ -237,7 +237,7 @@
         ],
         scratch_shapes=[pltpu.VMEM((block, LANES), F32)] * 3
         + [
-            pltpu.VMEM((high * plan["stride"], LANES), F32),
+            pltpu.VMEM(((high + 1) * plan["stride"], LANES), F32),
             pltpu.VMEM((high, channels, LANES), F32),
         ],
         compiler_params=pltpu.CompilerParams(vmem_limit_bytes=40 << 20),
@@ -354,7 +354,7 @@
         out_shape=jax.ShapeDtypeStruct((2 * LANES, width), BF),
         scratch_shapes=[pltpu.VMEM((block, LANES), F32)] * 3
         + [
-            pltpu.VMEM((high * plan["stride"], LANES), F32),
+            pltpu.VMEM(((high + 1) * plan["stride"], LANES), F32),
             pltpu.VMEM((block, channels), F32),
             pltpu.VMEM((high, channels, LANES), BF),
             pltpu.VMEM((2 * LANES, width), F32),

time: 276 us -> 277 us (level)
  no operation moved by 1% of the time
where the time goes in v1:
time: 277 us; the launch traced here: 275 us
  Pallas kernels  126 us (45%)
  starting transfers between devices  70.6 us (25%)
  waiting for transfers between devices  31.9 us (12%)
  blocking collectives  20.4 us (7%)
  local copies, waits for them, and re-layouts  13.2 us (5%)
  other arithmetic  11.4 us (4%)
    pallas_call x1, Pallas kernels, unpool(): pl.pallas_call(functools.partial(unpool_kernel, plan=plan), grid=(pixels...  50.6 us
    pallas_call x1, Pallas kernels, pool(): pl.pallas_call(functools.partial(pool_kernel, plan=plan), grid=(pixels //...  35.3 us
    ppermute x12, starting transfers between devices, moved(): lax.ppermute(tensor, 'strip', [(i, (i + 2 * shift) % strips) for i in ran...  22.3 us
    all_to_all x2, blocking collectives, shards(): shared = lax.all_to_all(sums, axes, 0, 0)  20.4 us
    pallas_call x2, Pallas kernels, taps(): pl.pallas_call(functools.partial(taps_kernel, widths=widths), in_specs=[p...  12.3 us
    all_to_all x2, starting transfers between devices, moments(): shared = lax.all_to_all(stats, ('batch', 'strip'), 0, 0)  12.2 us
    ppermute x5, waiting for transfers between devices, edges(): after = lax.ppermute(first, 'strip', [(j, i) for i, j in up])  11.3 us
    ppermute x5, starting transfers between devices, edges(): before = lax.ppermute(last, 'strip', up)  10.9 us
  transfers between devices with their start and end apart: 37, of which 14 were waited for; matrix products, arithmetic and copies ran while one was open for 4% of the time, Pallas kernels for 37%

profile of v1, /device:TPU:0, one launch (start us, length us, event | category | flops | bytes accessed | tf_op | source)
XLA Modules:
  0.0 275.4 jit_solution(5256121378987883549)
XLA Ops:
  2.0 3.1 %collective-permute-start = (bf16[9,32,640]{2,1,0:T(8,128)(2,1)S(1)}, bf16[9,32,640]{2,1,0:T(8,128)(2,1)S(1)}, u32[]{:S(2)}, u32[]{:S(2)}) collective-permute-start(bf16[9,32,640]{2,1,0:T(8,128)(2,1)S(1)} %fusion.4), channel_id=1, source_target_pairs={{0,2},{1,3},{2,4},{3,5},{4,6},{5,7},{6,0},{7,1},{8,10},{9,11},{10,... | collective-permute-start | bytes 1105928 | tf_op jit(solution)/shard_map/ppermute | solution.py:846
  5.1 2.6 collective-permute-start.1
  9.0 2.8 %copy.47 = s32[1,2112,118]{2,1,0:T(8,128)S(1)} copy(s32[1,2112,118]{1,0,2:T(1,128)} %param.25) | data formatting | bytes 1993728 | tf_op args[2]
  12.0 35.3 %pool.1 = (bf16[4,9,80,128]{3,2,1,0:T(8,128)(2,1)S(1)}, bf16[4,9,80,128]{3,2,1,0:T(8,128)(2,1)S(1)}, bf16[72,2112,128]{2,1,0:T(8,128)(2,1)}, bf16[256,256]{1,0:T(8,128)(2,1)S(1)}) custom-call(s32[3]{0:T(128)S(1)} %pad_add_fusion.place_ref, bf16[2112,256]{1,0:T(8,128)(2,1)S(1)} %bitcast.157, s32[2112,118]{1,0:T(8,128)S(1)} %bitcast.150, f32[198,256]{1,0:T(8,128)S(1)} %bitcast.155), custom_call_target="tpu_custom_call" | custom-call | flops 9965666304 | bytes 38928384 | tf_op jit(solution)/shard_map/pool/pallas_call | solution.py:217
  51.7 2.8 %collective-permute-start.6 = (bf16[9,80,128]{2,1,0:T(8,128)(2,1)}, bf16[9,80,128]{2,1,0:T(8,128)(2,1)}, u32[]{:S(2)}, u32[]{:S(2)}) collective-permute-start(bf16[9,80,128]{2,1,0:T(8,128)(2,1)} %get-tuple-element.182), channel_id=1, source_target_pairs={{0,6},{1,7},{2,0},{3,1},{4,2},{5,3},{6,4},{7,5},{8,14},{9,15},{10,... | collective-permute-start | bytes 552968 | tf_op jit(solution)/shard_map/ppermute | solution.py:846
  55.2 2.1 collective-permute-start.8
  59.8 2.8 %targets.1.refs_8_.gap_ref = f32[10,6,180]{2,1,0:T(8,128)} custom-call(s32[3,150]{1,0:T(4,128)} %bitcast.185, s32[1]{0:T(128)S(6)} %copy.65.count_ref, s32[1]{0:T(128)} %bitcast.16.first_ref), custom_call_target="tpu_custom_call" | custom-call | flops 1000 | bytes 1000 | tf_op jit(solution)/shard_map/targets/pallas_call | solution.py:61
  68.9 2.5 collective-permute-start.10
  72.8 4.6 %collective-permute-done.11.refs_7_.refs_5_ = bf16[1,180,128]{2,1,0:T(8,128)(2,1)S(1)} collective-permute-done((bf16[1,180,128]{2,1,0:T(8,128)(2,1)S(1)}, bf16[1,180,128]{2,1,0:T(8,128)(2,1)S(1)}, u32[]{:S(2)}, u32[]{:S(2)}) %collective-permute-start.11) | collective-permute-done | bytes 46112 | tf_op jit(solution)/shard_map/ppermute | solution.py:24
  78.7 4.4 %convolve.4 = (f32[6,180,256]{2,1,0:T(8,128)S(1)}, f32[32,3,256]{2,1,0:T(4,128)}) custom-call(bf16[9,256,256]{2,1,0:T(8,128)(2,1)S(1)} %copy-done.26, bf16[9,256,128]{2,1,0:T(8,128)(2,1)S(1)} %copy-done.30, bf16[1,180,256]{2,1,0:T(8,128)(2,1)} %collective-permute-done.8.refs_2_.refs_0_, bf16[6,180,256]{2,1,0:T(8,128)(2,1)S(1)} %bitcast.152, ...), custom_call_target="tpu_custom_call" | custom-call | flops 2038431744 | bytes 1769472 | tf_op jit(solution)/shard_map/convolve/pallas_call | solution.py:561
  83.2 5.4 %all-to-all-start = ((f32[32,3,256]{2,1,0:T(4,128)}), f32[32,3,256]{2,1,0:T(4,128)S(1)}, u32[]{:S(2)}, u32[]{:S(2)}) async-start(f32[32,3,256]{2,1,0:T(4,128)} %get-tuple-element.120), calls=%async_computation | async-start | bytes 262144 | tf_op jit(solution)/shard_map/all_to_all | solution.py:914
  88.6 2.2 collective-permute-start.12
  92.3 2.9 %collective-permute-done.13 = f32[1,180,256]{2,1,0:T(8,128)S(1)} collective-permute-done((f32[1,180,256]{2,1,0:T(8,128)S(1)}, f32[1,180,256]{2,1,0:T(8,128)S(1)}, u32[]{:S(2)}, u32[]{:S(2)}) %collective-permute-start.13) | collective-permute-done | bytes 184352 | tf_op jit(solution)/shard_map/ppermute | solution.py:24
  98.1 2.6 convolve.5
  100.7 6.8 %all-to-all-start.1 = ((f32[32,3,256]{2,1,0:T(4,128)}), f32[32,3,256]{2,1,0:T(4,128)S(1)}, u32[]{:S(2)}, u32[]{:S(2)}) async-start(f32[32,3,256]{2,1,0:T(4,128)} %get-tuple-element.126), calls=%async_computation.1 | async-start | bytes 262144 | tf_op jit(solution)/shard_map/all_to_all | solution.py:914
  108.3 7.3 %all-to-all-done.1 = f32[32,3,256]{2,1,0:T(4,128)S(1)} async-done(((f32[32,3,256]{2,1,0:T(4,128)}), f32[32,3,256]{2,1,0:T(4,128)S(1)}, u32[]{:S(2)}, u32[]{:S(2)}) %all-to-all-start.1) | async-done | bytes 98336 | tf_op jit(solution)/shard_map/all_to_all | solution.py:914
  115.8 3.1 %head.1 = (f32[6,180,256]{2,1,0:T(8,128)S(1)}, f32[32,2,256]{2,1,0:T(2,128)S(1)}, f32[1,1]{1,0:T(1,128)}, f32[11,256]{1,0:T(8,128)S(1)}) custom-call(f32[4,256]{1,0:T(4,128)S(1)} %pad_maximum_fusion.3.vector_ref, f32[6,180,256]{2,1,0:T(8,128)S(1)} %get-tuple-element.127.res_ref, bf16[6,180,256]{2,1,0:T(8,128)(2,1)S(1)} %multiply_convert_fusion.2.refs_2_.act_ref.refs_1_, ...), custom_call_target="tpu_custom_call" | custom-call | tf_op jit(solution)/shard_map/head/pallas_call | solution.py:536
  120.0 9.1 %all_to_all.30 = f32[32,2,256]{2,1,0:T(2,128)S(1)} all-to-all(f32[32,2,256]{2,1,0:T(2,128)S(1)} %get-tuple-element.129), channel_id=1, replica_groups=mesh['batch'=4,'strip'=8] {'batch','strip'}, dimensions={0} | all-to-all | bytes 131072 | tf_op jit(solution)/shard_map/all_to_all | solution.py:1054
  130.9 2.0 collective-permute-start.14
  136.1 2.1 convolve.6
  139.2 11.3 %all_to_all.31 = f32[32,2,256]{2,1,0:T(2,128)S(1)} all-to-all(f32[32,2,256]{2,1,0:T(2,128)S(1)} %get-tuple-element.131), channel_id=1, replica_groups=mesh['batch'=4,'strip'=8] {'batch','strip'}, dimensions={0} | all-to-all | bytes 131072 | tf_op jit(solution)/shard_map/all_to_all | solution.py:1072
  152.2 2.0 collective-permute-start.16
  159.2 3.0 %collective-permute-start.18 = (bf16[9,80,128]{2,1,0:T(8,128)(2,1)S(1)}, bf16[9,80,128]{2,1,0:T(8,128)(2,1)S(1)}, u32[]{:S(2)}, u32[]{:S(2)}) collective-permute-start(bf16[9,80,128]{2,1,0:T(8,128)(2,1)S(1)} %convolve.7), channel_id=1, source_target_pairs={{0,2},{1,3},{2,4},{3,5},{4,6},{5,7},{6,0},{7,1},{8,10},{9,11},{10,... | collective-permute-start | bytes 552968 | tf_op jit(solution)/shard_map/ppermute | solution.py:846
  165.1 5.3 %taps.3 = (bf16[4,9,32,256]{3,2,1,0:T(8,128)(2,1)S(1)}, bf16[4,9,32,256]{3,2,1,0:T(8,128)(2,1)}) custom-call(s32[3]{0:T(128)S(1)} %pad_add_fusion.place_ref, bf16[6,180,256]{2,1,0:T(8,128)(2,1)S(1)} %multiply_convert_fusion.1.refs_2_.grad_ref, bf16[1,180,256]{2,1,0:T(8,128)(2,1)S(1)} %copy-done.12, ...), custom_call_target="tpu_custom_call" | custom-call | flops 1000 | bytes 1000 | tf_op jit(solution)/shard_map/taps/pallas_call | solution.py:622
  170.4 7.0 %taps.2 = (bf16[4,9,32,336]{3,2,1,0:T(8,128)(2,1)S(1)}, bf16[4,9,32,336]{3,2,1,0:T(8,128)(2,1)S(1)}) custom-call(s32[3]{0:T(128)S(1)} %pad_add_fusion.place_ref, bf16[6,180,256]{2,1,0:T(8,128)(2,1)S(1)} %multiply_convert_fusion.refs_2_.grad_ref, bf16[1,180,256]{2,1,0:T(8,128)(2,1)} %collective-permute-done.8.refs_2_.refs_0_, ...), custom_call_target="tpu_custom_call" | custom-call | flops 1000 | bytes 1000 | tf_op jit(solution)/shard_map/taps/pallas_call | solution.py:622
  183.8 3.2 %collective-permute-start.24 = (bf16[9,32,592]{2,1,0:T(8,128)(2,1)S(1)}, bf16[9,32,592]{2,1,0:T(8,128)(2,1)S(1)}, u32[]{:S(2)}, u32[]{:S(2)}) collective-permute-start(bf16[9,32,592]{2,1,0:T(8,128)(2,1)S(1)} %get-tuple-element.178), channel_id=1, source_target_pairs={{0,2},{1,3},{2,4},{3,5},{4,6},{5,7},{6,0},{7,1},{8,10},{9,11},{10,... | collective-permute-start | bytes 1022984 | tf_op jit(solution)/shard_map/ppermute | solution.py:846
  189.5 50.6 %unpool.1 = bf16[256,256]{1,0:T(8,128)(2,1)} custom-call(s32[3]{0:T(128)S(1)} %pad_add_fusion.place_ref, bf16[2112,256]{1,0:T(8,128)(2,1)S(1)} %bitcast.158, s32[2112,118]{1,0:T(8,128)S(1)} %bitcast.151, bf16[256,256]{1,0:T(8,128)(2,1)S(1)} %copy-done.33, bf16[72,2112,128]{2,1,0:T(8,128)(2,1)} %get-tuple-element.99.dense_ref, ...), custom_call_target="tpu_custom_call" | custom-call | flops 14948499456 | bytes 38928384 | tf_op jit(solution)/shard_map/unpool/pallas_call | solution.py:340
  240.1 2.6 all-to-all-start.4
  247.6 2.7 collective-permute-done.27.refs_1_
  253.4 4.6 %all-to-all-start.5 = ((bf16[32,8,384]{2,1,0:T(8,128)(2,1)}), bf16[32,8,384]{2,1,0:T(8,128)(2,1)S(1)}, u32[]{:S(2)}, u32[]{:S(2)}) async-start(bf16[32,8,384]{2,1,0:T(8,128)(2,1)} %get-tuple-element.154), calls=%async_computation.5 | async-start | bytes 393216 | tf_op jit(solution)/shard_map/all_to_all | solution.py:1128
  263.4 2.4 collective-permute-done.30.refs_1_
  268.3 5.9 %update.1 = (f32[1,1]{1,0:T(1,128)}, f32[1,128]{1,0:T(1,128)}, f32[198,256]{1,0:T(8,128)}, f32[198,256]{1,0:T(8,128)}, f32[198,256]{1,0:T(8,128)}, /*index=5*/f3...) custom-call(s32[3]{0:T(128)} %copy-done.21, ...), custom_call_target="tpu_custom_call" | custom-call | tf_op jit(solution)/shard_map/update/pallas_call | solution.py:814
  (192 shorter events, 65.9 us)
Async XLA Ops:
  2.0 45.3 %collective-permute-start = (bf16[9,32,640]{2,1,0:T(8,128)(2,1)S(1)}, bf16[9,32,640]{2,1,0:T(8,128)(2,1)S(1)}, u32[]{:S(2)}, u32[]{:S(2)}) collective-permute-start(bf16[9,32,640]{2,1,0:T(8,128)(2,1)S(1)} %fusion.4), channel_id=1, source_target_pairs={{0,2},{1,3},{2,4},{3,5},{4,6},{5,7},{6,0},{7,1},{8,10},{9,11},{10,... | collective-permute-start | bytes 1105928 | tf_op jit(solution)/shard_map/ppermute | solution.py:846
  5.1 42.2 %collective-permute-start.1 = (bf16[9,32,640]{2,1,0:T(8,128)(2,1)S(1)}, bf16[9,32,640]{2,1,0:T(8,128)(2,1)S(1)}, u32[]{:S(2)}, u32[]{:S(2)}) collective-permute-start(bf16[9,32,640]{2,1,0:T(8,128)(2,1)S(1)} %fusion.4), channel_id=1, source_target_pairs={{0,4},{1,5},{2,6},{3,7},{4,0},{5,1},{6,2},{7,3},{8,12},{9,13},{10,... | collective-permute-start | bytes 1105928 | tf_op jit(solution)/shard_map/ppermute | solution.py:846
  7.7 39.6 %collective-permute-start.2 = (bf16[9,32,640]{2,1,0:T(8,128)(2,1)S(1)}, bf16[9,32,640]{2,1,0:T(8,128)(2,1)}, u32[]{:S(2)}, u32[]{:S(2)}) collective-permute-start(bf16[9,32,640]{2,1,0:T(8,128)(2,1)S(1)} %fusion.4), channel_id=1, source_target_pairs={{0,6},{1,7},{2,0},{3,1},{4,2},{5,3},{6,4},{7,5},{8,14},{9,15},{10,... | collective-permute-start | bytes 1105928 | tf_op jit(solution)/shard_map/ppermute | solution.py:846
  48.6 8.7 %collective-permute-start.7 = (bf16[4,9,32,640]{3,2,1,0:T(8,128)(2,1)S(1)}, bf16[4,9,32,640]{3,2,1,0:T(8,128)(2,1)S(1)}, u32[]{:S(2)}, u32[]{:S(2)}) collective-permute-start(bf16[4,9,32,640]{3,2,1,0:T(8,128)(2,1)S(1)} %pad_maximum_fusion.mine_ref), channel_id=1, source_target_pairs={{0,1},{1,0},{2,3},{3,2},{4,5},{5,4},{6,7},{7,6},{8,9},{9,8},{10,11... | collective-permute-start | bytes 4423688 | tf_op jit(solution)/shard_map/ppermute | solution.py:837
  50.7 15.9 %collective-permute-start.4 = (bf16[9,80,128]{2,1,0:T(8,128)(2,1)}, bf16[9,80,128]{2,1,0:T(8,128)(2,1)}, u32[]{:S(2)}, u32[]{:S(2)}) collective-permute-start(bf16[9,80,128]{2,1,0:T(8,128)(2,1)} %get-tuple-element.184), channel_id=1, source_target_pairs={{0,2},{1,3},{2,4},{3,5},{4,6},{5,7},{6,0},{7,1},{8,10},{9,11},{10,... | collective-permute-start | bytes 552968 | tf_op jit(solution)/shard_map/ppermute | solution.py:846
  51.3 16.2 %collective-permute-start.5 = (bf16[9,80,128]{2,1,0:T(8,128)(2,1)}, bf16[9,80,128]{2,1,0:T(8,128)(2,1)}, u32[]{:S(2)}, u32[]{:S(2)}) collective-permute-start(bf16[9,80,128]{2,1,0:T(8,128)(2,1)} %get-tuple-element.183), channel_id=1, source_target_pairs={{0,4},{1,5},{2,6},{3,7},{4,0},{5,1},{6,2},{7,3},{8,12},{9,13},{10,... | collective-permute-start | bytes 552968 | tf_op jit(solution)/shard_map/ppermute | solution.py:846
  51.7 15.9 %collective-permute-start.6 = (bf16[9,80,128]{2,1,0:T(8,128)(2,1)}, bf16[9,80,128]{2,1,0:T(8,128)(2,1)}, u32[]{:S(2)}, u32[]{:S(2)}) collective-permute-start(bf16[9,80,128]{2,1,0:T(8,128)(2,1)} %get-tuple-element.182), channel_id=1, source_target_pairs={{0,6},{1,7},{2,0},{3,1},{4,2},{5,3},{6,4},{7,5},{8,14},{9,15},{10,... | collective-permute-start | bytes 552968 | tf_op jit(solution)/shard_map/ppermute | solution.py:846
  55.2 11.3 %collective-permute-start.8 = (bf16[1,180,256]{2,1,0:T(8,128)(2,1)}, bf16[1,180,256]{2,1,0:T(8,128)(2,1)}, u32[]{:S(2)}, u32[]{:S(2)}) collective-permute-start(bf16[1,180,256]{2,1,0:T(8,128)(2,1)} %get-tuple-element.191), channel_id=1, source_target_pairs={{0,1},{1,2},{2,3},{3,4},{4,5},{5,6},{6,7},{8,9},{9,10},{10,11},{11... | collective-permute-start | bytes 276488 | tf_op jit(solution)/shard_map/ppermute | solution.py:23
  57.3 9.2 %collective-permute-start.9 = (bf16[1,180,256]{2,1,0:T(8,128)(2,1)}, bf16[1,180,256]{2,1,0:T(8,128)(2,1)}, u32[]{:S(2)}, u32[]{:S(2)}) collective-permute-start(bf16[1,180,256]{2,1,0:T(8,128)(2,1)} %get-tuple-element.190), channel_id=1, source_target_pairs={{1,0},{2,1},{3,2},{4,3},{5,4},{6,5},{7,6},{9,8},{10,9},{11,10},{12... | collective-permute-start | bytes 276488 | tf_op jit(solution)/shard_map/ppermute | solution.py:24
  68.9 3.9 %collective-permute-start.10 = (bf16[1,180,128]{2,1,0:T(8,128)(2,1)S(1)}, bf16[1,180,128]{2,1,0:T(8,128)(2,1)S(1)}, u32[]{:S(2)}, u32[]{:S(2)}) collective-permute-start(bf16[1,180,128]{2,1,0:T(8,128)(2,1)S(1)} %get-tuple-element.197), channel_id=1, source_target_pairs={{0,1},{1,2},{2,3},{3,4},{4,5},{5,6},{6,7},{8,9},{9,10},{10,11},{11... | collective-permute-start | bytes 138248 | tf_op jit(solution)/shard_map/ppermute | solution.py:23
  71.4 6.0 %collective-permute-start.11 = (bf16[1,180,128]{2,1,0:T(8,128)(2,1)S(1)}, bf16[1,180,128]{2,1,0:T(8,128)(2,1)S(1)}, u32[]{:S(2)}, u32[]{:S(2)}) collective-permute-start(bf16[1,180,128]{2,1,0:T(8,128)(2,1)S(1)} %get-tuple-element.196), channel_id=1, source_target_pairs={{1,0},{2,1},{3,2},{4,3},{5,4},{6,5},{7,6},{9,8},{10,9},{11,10},{12... | collective-permute-start | bytes 138248 | tf_op jit(solution)/shard_map/ppermute | solution.py:24
  83.2 13.6 %all-to-all-start = ((f32[32,3,256]{2,1,0:T(4,128)}), f32[32,3,256]{2,1,0:T(4,128)S(1)}, u32[]{:S(2)}, u32[]{:S(2)}) async-start(f32[32,3,256]{2,1,0:T(4,128)} %get-tuple-element.120), calls=%async_computation | async-start | bytes 262144 | tf_op jit(solution)/shard_map/all_to_all | solution.py:914
  88.6 3.7 %collective-permute-start.12 = (f32[1,180,256]{2,1,0:T(8,128)S(1)}, f32[1,180,256]{2,1,0:T(8,128)S(1)}, u32[]{:S(2)}, u32[]{:S(2)}) collective-permute-start(f32[1,180,256]{2,1,0:T(8,128)S(1)} %get-tuple-element.181), channel_id=1, source_target_pairs={{0,1},{1,2},{2,3},{3,4},{4,5},{5,6},{6,7},{8,9},{9,10},{10,11},{11... | collective-permute-start | bytes 552968 | tf_op jit(solution)/shard_map/ppermute | solution.py:23
  90.8 4.5 %collective-permute-start.13 = (f32[1,180,256]{2,1,0:T(8,128)S(1)}, f32[1,180,256]{2,1,0:T(8,128)S(1)}, u32[]{:S(2)}, u32[]{:S(2)}) collective-permute-start(f32[1,180,256]{2,1,0:T(8,128)S(1)} %get-tuple-element.180), channel_id=1, source_target_pairs={{1,0},{2,1},{3,2},{4,3},{5,4},{6,5},{7,6},{9,8},{10,9},{11,10},{12... | collective-permute-start | bytes 552968 | tf_op jit(solution)/shard_map/ppermute | solution.py:24
  100.7 15.0 %all-to-all-start.1 = ((f32[32,3,256]{2,1,0:T(4,128)}), f32[32,3,256]{2,1,0:T(4,128)S(1)}, u32[]{:S(2)}, u32[]{:S(2)}) async-start(f32[32,3,256]{2,1,0:T(4,128)} %get-tuple-element.126), calls=%async_computation.1 | async-start | bytes 262144 | tf_op jit(solution)/shard_map/all_to_all | solution.py:914
  152.2 3.5 %collective-permute-start.16 = (bf16[1,180,256]{2,1,0:T(8,128)(2,1)S(1)}, bf16[1,180,256]{2,1,0:T(8,128)(2,1)S(1)}, u32[]{:S(2)}, u32[]{:S(2)}) collective-permute-start(bf16[1,180,256]{2,1,0:T(8,128)(2,1)S(1)} %get-tuple-element.187), channel_id=1, source_target_pairs={{0,1},{1,2},{2,3},{3,4},{4,5},{5,6},{6,7},{8,9},{9,10},{10,11},{11... | collective-permute-start | bytes 276488 | tf_op jit(solution)/shard_map/ppermute | solution.py:23
  159.2 18.2 %collective-permute-start.18 = (bf16[9,80,128]{2,1,0:T(8,128)(2,1)S(1)}, bf16[9,80,128]{2,1,0:T(8,128)(2,1)S(1)}, u32[]{:S(2)}, u32[]{:S(2)}) collective-permute-start(bf16[9,80,128]{2,1,0:T(8,128)(2,1)S(1)} %convolve.7), channel_id=1, source_target_pairs={{0,2},{1,3},{2,4},{3,5},{4,6},{5,7},{6,0},{7,1},{8,10},{9,11},{10,... | collective-permute-start | bytes 552968 | tf_op jit(solution)/shard_map/ppermute | solution.py:846
  162.3 15.1 %collective-permute-start.19 = (bf16[9,80,128]{2,1,0:T(8,128)(2,1)S(1)}, bf16[9,80,128]{2,1,0:T(8,128)(2,1)S(1)}, u32[]{:S(2)}, u32[]{:S(2)}) collective-permute-start(bf16[9,80,128]{2,1,0:T(8,128)(2,1)S(1)} %convolve.7), channel_id=1, source_target_pairs={{0,4},{1,5},{2,6},{3,7},{4,0},{5,1},{6,2},{7,3},{8,12},{9,13},{10,... | collective-permute-start | bytes 552968 | tf_op jit(solution)/shard_map/ppermute | solution.py:846
  163.2 14.3 %collective-permute-start.20 = (bf16[9,80,128]{2,1,0:T(8,128)(2,1)S(1)}, bf16[9,80,128]{2,1,0:T(8,128)(2,1)S(1)}, u32[]{:S(2)}, u32[]{:S(2)}) collective-permute-start(bf16[9,80,128]{2,1,0:T(8,128)(2,1)S(1)} %convolve.7), channel_id=1, source_target_pairs={{0,6},{1,7},{2,0},{3,1},{4,2},{5,3},{6,4},{7,5},{8,14},{9,15},{10,... | collective-permute-start | bytes 552968 | tf_op jit(solution)/shard_map/ppermute | solution.py:846
  178.1 4.1 %collective-permute-start.23 = (bf16[4,9,32,336]{3,2,1,0:T(8,128)(2,1)S(1)}, bf16[4,9,32,336]{3,2,1,0:T(8,128)(2,1)}, u32[]{:S(2)}, u32[]{:S(2)}) collective-permute-start(bf16[4,9,32,336]{3,2,1,0:T(8,128)(2,1)S(1)} %get-tuple-element.147), channel_id=1, source_target_pairs={{0,1},{1,0},{2,3},{3,2},{4,5},{5,4},{6,7},{7,6},{8,9},{9,8},{10,11... | collective-permute-start | bytes 2322440 | tf_op jit(solution)/shard_map/ppermute | solution.py:837
  178.3 11.2 %collective-permute-start.21 = (bf16[4,9,80,128]{3,2,1,0:T(8,128)(2,1)S(1)}, bf16[4,9,80,128]{3,2,1,0:T(8,128)(2,1)S(1)}, u32[]{:S(2)}, u32[]{:S(2)}) collective-permute-start(bf16[4,9,80,128]{3,2,1,0:T(8,128)(2,1)S(1)} %pad_maximum_fusion.1.mine_ref), channel_id=1, source_target_pairs={{0,1},{1,0},{2,3},{3,2},{4,5},{5,4},{6,7},{7,6},{8,9},{9,8},{10,11... | collective-permute-start | bytes 2211848 | tf_op jit(solution)/shard_map/ppermute | solution.py:837
  183.8 56.3 %collective-permute-start.24 = (bf16[9,32,592]{2,1,0:T(8,128)(2,1)S(1)}, bf16[9,32,592]{2,1,0:T(8,128)(2,1)S(1)}, u32[]{:S(2)}, u32[]{:S(2)}) collective-permute-start(bf16[9,32,592]{2,1,0:T(8,128)(2,1)S(1)} %get-tuple-element.178), channel_id=1, source_target_pairs={{0,2},{1,3},{2,4},{3,5},{4,6},{5,7},{6,0},{7,1},{8,10},{9,11},{10,... | collective-permute-start | bytes 1022984 | tf_op jit(solution)/shard_map/ppermute | solution.py:846
  187.0 53.1 %collective-permute-start.25 = (bf16[9,32,592]{2,1,0:T(8,128)(2,1)S(1)}, bf16[9,32,592]{2,1,0:T(8,128)(2,1)S(1)}, u32[]{:S(2)}, u32[]{:S(2)}) collective-permute-start(bf16[9,32,592]{2,1,0:T(8,128)(2,1)S(1)} %get-tuple-element.179), channel_id=1, source_target_pairs={{0,4},{1,5},{2,6},{3,7},{4,0},{5,1},{6,2},{7,3},{8,12},{9,13},{10,... | collective-permute-start | bytes 1022984 | tf_op jit(solution)/shard_map/ppermute | solution.py:846
  188.9 51.3 %collective-permute-start.26 = (bf16[9,32,592]{2,1,0:T(8,128)(2,1)S(1)}, bf16[9,32,592]{2,1,0:T(8,128)(2,1)S(1)}, u32[]{:S(2)}, u32[]{:S(2)}) collective-permute-start(bf16[9,32,592]{2,1,0:T(8,128)(2,1)S(1)} %get-tuple-element.176), channel_id=1, source_target_pairs={{0,6},{1,7},{2,0},{3,1},{4,2},{5,3},{6,4},{7,5},{8,14},{9,15},{10,... | collective-permute-start | bytes 1022984 | tf_op jit(solution)/shard_map/ppermute | solution.py:846
  240.1 11.6 %all-to-all-start.4 = ((bf16[32,8,256]{2,1,0:T(8,128)(2,1)}), bf16[32,8,256]{2,1,0:T(8,128)(2,1)S(1)}, u32[]{:S(2)}, u32[]{:S(2)}) async-start(bf16[32,8,256]{2,1,0:T(8,128)(2,1)} %bitcast.49), calls=%async_computation.4 | async-start | bytes 262144 | tf_op jit(solution)/shard_map/all_to_all | solution.py:1126
  243.0 7.3 %collective-permute-start.27 = (bf16[72,592]{1,0:T(8,128)(2,1)S(1)}, bf16[72,592]{1,0:T(8,128)(2,1)S(1)}, u32[]{:S(2)}, u32[]{:S(2)}) collective-permute-start(bf16[72,592]{1,0:T(8,128)(2,1)S(1)} %get-tuple-element.194), channel_id=1, source_target_pairs={{0,8},{8,16},{16,24},{24,0},{1,9},{9,17},{17,25},{25,1},{2,10},{10... | collective-permute-start | bytes 255752 | tf_op jit(solution)/shard_map/ppermute | solution.py:927
  244.7 7.0 %collective-permute-start.28 = (bf16[72,592]{1,0:T(8,128)(2,1)S(1)}, bf16[72,592]{1,0:T(8,128)(2,1)S(1)}, u32[]{:S(2)}, u32[]{:S(2)}) collective-permute-start(bf16[72,592]{1,0:T(8,128)(2,1)S(1)} %get-tuple-element.193), channel_id=1, source_target_pairs={{0,16},{8,24},{16,0},{24,8},{1,17},{9,25},{17,1},{25,9},{2,18},{10... | collective-permute-start | bytes 255752 | tf_op jit(solution)/shard_map/ppermute | solution.py:927
  246.2 5.5 %collective-permute-start.29 = (bf16[72,592]{1,0:T(8,128)(2,1)S(1)}, bf16[72,592]{1,0:T(8,128)(2,1)S(1)}, u32[]{:S(2)}, u32[]{:S(2)}) collective-permute-start(bf16[72,592]{1,0:T(8,128)(2,1)S(1)} %get-tuple-element.192), channel_id=1, source_target_pairs={{0,24},{8,0},{16,8},{24,16},{1,25},{9,1},{17,9},{25,17},{2,26},{10... | collective-permute-start | bytes 255752 | tf_op jit(solution)/shard_map/ppermute | solution.py:927
  253.4 14.2 %all-to-all-start.5 = ((bf16[32,8,384]{2,1,0:T(8,128)(2,1)}), bf16[32,8,384]{2,1,0:T(8,128)(2,1)S(1)}, u32[]{:S(2)}, u32[]{:S(2)}) async-start(bf16[32,8,384]{2,1,0:T(8,128)(2,1)} %get-tuple-element.154), calls=%async_computation.5 | async-start | bytes 393216 | tf_op jit(solution)/shard_map/all_to_all | solution.py:1128
  258.0 7.7 %collective-permute-start.30 = (bf16[72,592]{1,0:T(8,128)(2,1)S(1)}, bf16[72,592]{1,0:T(8,128)(2,1)S(1)}, u32[]{:S(2)}, u32[]{:S(2)}) collective-permute-start(bf16[72,592]{1,0:T(8,128)(2,1)S(1)} %get-tuple-element.155.refs_0_), channel_id=1, source_target_pairs={{0,8},{8,16},{16,24},{24,0},{1,9},{9,17},{17,25},{25,1},{2,10},{10... | collective-permute-start | bytes 255752 | tf_op jit(solution)/shard_map/ppermute | solution.py:927
  259.8 7.7 %collective-permute-start.31 = (bf16[72,592]{1,0:T(8,128)(2,1)S(1)}, bf16[72,592]{1,0:T(8,128)(2,1)S(1)}, u32[]{:S(2)}, u32[]{:S(2)}) collective-permute-start(bf16[72,592]{1,0:T(8,128)(2,1)S(1)} %get-tuple-element.155.refs_0_), channel_id=1, source_target_pairs={{0,16},{8,24},{16,0},{24,8},{1,17},{9,25},{17,1},{25,9},{2,18},{10... | collective-permute-start | bytes 255752 | tf_op jit(solution)/shard_map/ppermute | solution.py:927
  261.3 6.3 %collective-permute-start.32 = (bf16[72,592]{1,0:T(8,128)(2,1)S(1)}, bf16[72,592]{1,0:T(8,128)(2,1)S(1)}, u32[]{:S(2)}, u32[]{:S(2)}) collective-permute-start(bf16[72,592]{1,0:T(8,128)(2,1)S(1)} %get-tuple-element.155.refs_0_), channel_id=1, source_target_pairs={{0,24},{8,0},{16,8},{24,16},{1,25},{9,1},{17,9},{25,17},{2,26},{10... | collective-permute-start | bytes 255752 | tf_op jit(solution)/shard_map/ppermute | solution.py:927
  (48 other events, 501.5 us)
